TPU v7x, 256 devices: a whole 4x4x8 slice. The times are simulated.
256 devices in a mesh: pts: 16 (over x_hi, z), fn: 16 (over x_lo, y, core).
Axes of the slice: x: 4 (x_hi: 2, x_lo: 2; x = x_hi * 2 + x_lo), y: 4, z: 8, core: 2. Of those that a mesh axis runs over, the one named last changes fastest.
Arguments:
- grad_out: bfloat16 [128, 131072], P('fn', 'pts'), may hold values from -0.0390625 to 0.0390625
- coef: bfloat16 [128, 512], P('fn'), may hold values from -0.5 to 0.5
- coords: float32 [3, 131072], P(None, 'pts'), may hold values from -1 to 1
- w_first: float32 [3, 512], replicated, may hold values from -3.5 to 3.5
- b_first: float32 [512], replicated, may hold values from -3 to 3
- w_second: bfloat16 [512, 512], replicated, may hold values from -0.25 to 0.25
- b_second: float32 [512], replicated, may hold values from -3 to 3
- w_third: bfloat16 [512, 512], replicated, may hold values from -0.25 to 0.25
- b_third: float32 [512], replicated, may hold values from -4 to 4
Outputs:
- grad_coef: float32 [128, 512], P('fn', 'pts')
- grad_w_first: float32 [3, 512], replicated
- grad_b_first: float32 [512], replicated
- grad_w_second: float32 [512, 512], replicated
- grad_b_second: float32 [512], replicated
- grad_w_third: float32 [512, 512], replicated
- grad_b_third: float32 [512], replicated
All inputs are finite; a program needn't handle non-finite values.
Results may differ from a plain program's by a relative error of at most 0.012.
The roundings to bfloat16 on the way count: a program that leaves them out, or rounds other values in their place, can miss the bound.
Values may be sent and summed in bfloat16 or wider, within the bound.
No kernel may reach another device: no remote copies, remote signals or barrier semaphores. Data moves between devices by JAX's collectives and lax.ppermute only.
A program may use at most 128 MiB of HBM per device.

v0:
```python
import jax
import jax.numpy as jnp
from jax import lax
from jax.sharding import PartitionSpec as P


def trunk_forward(points, w_first, b_first, w_second, b_second, w_third, b_third):
    z_one = (
        jnp.dot(
            points.T, w_first, precision=lax.Precision.HIGHEST, preferred_element_type=jnp.float32
        )
        + b_first
    )
    act_one = jnp.tanh(z_one).astype(jnp.bfloat16)
    act_two = jnp.tanh(
        jnp.dot(act_one, w_second, preferred_element_type=jnp.float32) + b_second
    ).astype(jnp.bfloat16)
    basis = (jnp.dot(act_two, w_third, preferred_element_type=jnp.float32) + b_third).astype(
        jnp.bfloat16
    )
    return (act_one, act_two, basis)


def trunk_backward(points, act_one, act_two, grad_basis, w_second, w_third):
    grad_w_third = jnp.dot(act_two.T, grad_basis, preferred_element_type=jnp.float32)
    grad_b_third = jnp.sum(grad_basis.astype(jnp.float32), axis=0)
    two_f = act_two.astype(jnp.float32)
    pre_two = (
        jnp.dot(grad_basis, w_third.T, preferred_element_type=jnp.float32) * (1.0 - two_f * two_f)
    ).astype(jnp.bfloat16)
    grad_w_second = jnp.dot(act_one.T, pre_two, preferred_element_type=jnp.float32)
    grad_b_second = jnp.sum(pre_two.astype(jnp.float32), axis=0)
    one_f = act_one.astype(jnp.float32)
    pre_one = jnp.dot(pre_two, w_second.T, preferred_element_type=jnp.float32) * (
        1.0 - one_f * one_f
    )
    grad_w_first = jnp.dot(
        points, pre_one, precision=lax.Precision.HIGHEST, preferred_element_type=jnp.float32
    )
    grad_b_first = jnp.sum(pre_one, axis=0)
    return (grad_w_first, grad_b_first, grad_w_second, grad_b_second, grad_w_third, grad_b_third)


def shards(grad_out, coef, coords, w_first, b_first, w_second, b_second, w_third, b_third):
    share = grad_out.shape[1] // lax.axis_size("fn")
    offset = lax.axis_index("fn") * share
    own_points = lax.dynamic_slice_in_dim(coords, offset, share, 1)
    act_one, act_two, basis = trunk_forward(
        coords, w_first, b_first, w_second, b_second, w_third, b_third
    )
    partial_value = jnp.dot(grad_out, basis, preferred_element_type=jnp.float32)
    grad_basis = lax.psum_scatter(
        lax.dot_general(
            grad_out, coef, (((0,), (0,)), ((), ())), preferred_element_type=jnp.float32
        ),
        "fn",
        scatter_dimension=0,
        tiled=True,
    ).astype(jnp.bfloat16)
    own_one = lax.dynamic_slice_in_dim(act_one, offset, share, 0)
    own_two = lax.dynamic_slice_in_dim(act_two, offset, share, 0)
    grads = trunk_backward(own_points, own_one, own_two, grad_basis, w_second, w_third)
    grad_coef = lax.psum_scatter(partial_value, "pts", scatter_dimension=1, tiled=True)
    summed = lax.psum((grads[0], grads[1], grads[2], grads[3], grads[4], grads[5]), ("pts", "fn"))
    return (grad_coef, summed[0], summed[1], summed[2], summed[3], summed[4], summed[5])


def solution(mesh):
    return jax.shard_map(
        shards,
        mesh=mesh,
        in_specs=(P("fn", "pts"), P("fn", None), P(None, "pts"), P(), P(), P(), P(), P(), P()),
        out_specs=(P("fn", "pts"), P(), P(), P(), P(), P(), P()),
        check_vma=False,
    )
```

profile of v0, /device:TPU:1, one launch (start us, length us, event | category | flops | bytes accessed | tf_op | source)
XLA Modules:
  0.0 596.8 jit_solution(12960392394778353244)
XLA Ops:
  7.2 0.0 copy-start
  7.2 0.0 reduce-scatter.5.cloned.1.call-start
  7.2 9.1 %fusion.15 = f32[8192,512]{1,0:T(8,128)} fusion(bf16[8,8192]{1,0:T(8,128)(2,1)} %param.9, bf16[8,512]{1,0:T(8,128)(2,1)} %param.10), kind=kOutput, calls=%fused_computation.22 | convolution fusion | flops 67108864 | bytes 16916480 | tf_op jit(solution)/shard_map/dot_general | solution.py:53
  16.3 0.0 reduce-scatter.5.cloned.1.call-update
  16.3 0.0 copy-start.8
  16.3 0.0 reduce-scatter.7.cloned.1.call-start
  16.4 0.8 copy-done.5
  17.2 0.0 copy-done.6
  17.2 14.6 %tanh_convert_fusion.1 = bf16[8192,512]{1,0:T(8,128)(2,1)S(1)} fusion(f32[3,8192]{1,0:T(4,128)S(1)} %copy-done.5, f32[3,512]{1,0:T(4,128)S(1)} %copy-done.6, f32[512]{0:T(512)S(1)} %copy-done.7), kind=kOutput, calls=%fused_computation.2 | convolution fusion | flops 159383552 | bytes 8495104 | tf_op jit(solution)/shard_map/dot_general | solution.py:9
  31.8 0.0 copy-start.4
  31.8 3.2 copy-done.4
  35.0 0.0 copy-done
  35.0 0.0 copy-start.9
  35.0 6.7 %tanh_convert_fusion = bf16[8192,512]{1,0:T(8,128)(2,1)} fusion(bf16[8192,512]{1,0:T(8,128)(2,1)S(1)} %tanh_convert_fusion.1, bf16[512,512]{1,0:T(8,128)(2,1)S(1)} %copy-done, f32[512]{0:T(512)S(1)} %copy-done.8), kind=kOutput, calls=%fused_computation.1 | convolution fusion | flops 4303355904 | bytes 17303552 | tf_op jit(solution)/shard_map/dot_general | solution.py:16
  41.7 8.0 %fusion.2 = f32[8,512]{1,0:T(8,128)S(1)} fusion(bf16[8,8192]{1,0:T(8,128)(2,1)S(1)} %copy-done.3, bf16[8192,512]{1,0:T(8,128)(2,1)} %tanh_convert_fusion, bf16[512,512]{1,0:T(8,128)(2,1)S(1)} %copy-done.2, f32[512]{0:T(512)S(1)} %copy-done.9), kind=kOutput, calls=%fused_computation.7 | convolution fusion | flops 4370464768 | bytes 9062400 | tf_op jit(solution)/shard_map/dot_general | solution.py:51
  49.7 0.9 copy.16
  50.5 0.0 reduce-scatter.7.cloned.1.call-update
  50.6 0.2 all-reduce.4.cloned.1.call-start
  50.8 68.8 %reduce-scatter.5.cloned.1.call-done = f32[512,512]{1,0:T(8,128)} async-done(((f32[8192,512]{1,0:T(8,128)}), f32[512,512]{1,0:T(8,128)}) %reduce-scatter.5.cloned.1.call-update) | async-done | bytes 1048592 | tf_op jit(solution)/shard_map/reduce_scatter | solution.py:52
  119.6 2.0 convert_reduce_fusion.1
  121.6 2.8 fusion.5
  124.4 2.5 fusion.3
  126.9 0.0 all-reduce.4.cloned.1.call-update
  126.9 187.9 %reduce-scatter.7.cloned.1.call-done = f32[32,8]{1,0:T(8,128)} async-done(((f32[512,8]{1,0:T(8,128)}), f32[32,8]{1,0:T(8,128)}) %reduce-scatter.7.cloned.1.call-update) | async-done | bytes 1040
  314.8 1.4 copy.17
  316.2 0.1 convert_reduce_fusion
  316.3 1.5 fusion.14
  317.8 0.6 fusion.7
  318.4 79.9 %all-reduce = (f32[3,512]{1,0:T(4,128)}, f32[512]{0:T(512)}, f32[512]{0:T(512)}, f32[512]{0:T(512)}) all-reduce(f32[3,512]{1,0:T(4,128)S(1)} %fusion.7, f32[512]{0:T(512)S(1)} %get-tuple-element.13, f32[512]{0:T(512)S(1)} %get-tuple-element.15, f32[512]{0:T(512)S(1)} %convert_reduce_fusion), channel_id=1, replica_groups=mesh['pts'=16,'fn'=16] {'pts','fn'}, use_global_device_ids=true, to_apply=%region_2.0 | all-reduce | flops 3072 | bytes 24576 | tf_op jit(solution)/shard_map/psum | solution.py:64
  398.3 187.4 %all-reduce.4.cloned.1.call-done = (f32[512,512]{1,0:T(8,128)}, f32[512,512]{1,0:T(8,128)}) async-done(((f32[512,512]{1,0:T(8,128)}, f32[512,512]{1,0:T(8,128)}), (f32[512,512]{1,0:T(8,128)}, f32[512,512]{1,0:T(8,128)})) %all-reduce.4.cloned.1.call-update) | async-done | bytes 2097168 | tf_op jit(solution)/shard_map/psum | solution.py:64
  585.7 2.3 copy.20
  588.0 2.3 copy.21
  (12 shorter events, 0.0 us)
Async XLA Ops:
  7.2 27.9 %copy-start = (bf16[512,512]{1,0:T(8,128)(2,1)S(1)}, bf16[512,512]{1,0:T(8,128)(2,1)}, u32[]{:S(2)}) copy-start(bf16[512,512]{1,0:T(8,128)(2,1)} %param.14) | copy-start | bytes 1572868
  7.2 112.4 %reduce-scatter.5.cloned.1.call-start = ((), (), s32[]{:S(2)}) async-start(), calls=%async_computation.2 | async-start | bytes 17825792 | tf_op jit(solution)/shard_map/reduce_scatter | solution.py:52
  16.3 0.9 copy-start.5
  16.3 0.9 copy-start.6
  16.3 0.9 copy-start.7
  16.3 18.7 %copy-start.8 = (f32[512]{0:T(512)S(1)}, f32[512]{0:T(512)}, u32[]{:S(2)}) copy-start(f32[512]{0:T(512)} %param.15) | copy-start | bytes 6148
  16.3 298.5 %reduce-scatter.7.cloned.1.call-start = ((), (), s32[]{:S(2)}) async-start(), calls=%async_computation.3 | async-start | bytes 278528
  31.8 3.2 copy-start.4
  35.0 6.7 %copy-start.2 = (bf16[512,512]{1,0:T(8,128)(2,1)S(1)}, bf16[512,512]{1,0:T(8,128)(2,1)}, u32[]{:S(2)}) copy-start(bf16[512,512]{1,0:T(8,128)(2,1)} %param.16) | copy-start | bytes 1572868
  35.0 6.7 %copy-start.3 = (bf16[8,8192]{1,0:T(8,128)(2,1)S(1)}, bf16[8,8192]{1,0:T(8,128)(2,1)}, u32[]{:S(2)}) copy-start(bf16[8,8192]{1,0:T(8,128)(2,1)} %param.9) | copy-start | bytes 393220
  35.0 6.7 %copy-start.9 = (f32[512]{0:T(512)S(1)}, f32[512]{0:T(512)}, u32[]{:S(2)}) copy-start(f32[512]{0:T(512)} %param.17) | copy-start | bytes 6148
  50.6 535.2 %all-reduce.4.cloned.1.call-start = ((), (), s32[]{:S(2)}) async-start(), calls=%async_computation.4 | async-start | bytes 4194304 | tf_op jit(solution)/shard_map/psum | solution.py:64
  119.6 196.5 %copy-start.1 = (f32[512,512]{1,0:T(8,128)S(1)}, f32[512,512]{1,0:T(8,128)}, u32[]{:S(2)}) copy-start(f32[512,512]{1,0:T(8,128)} %reduce-scatter.5.cloned.1.call-done) | copy-start | bytes 3145732
Sparse Core Ops, SparseCore 0:
  16.4 103.1 reduce-scatter.4
  123.4 191.3 reduce-scatter.6
  321.8 263.8 all-reduce.3
where the time goes:
time: 598 us; the launch traced here: 597 us
  waiting for transfers between devices  444 us (74%)
  blocking collectives  79.9 us (13%)
  matrix products  47.7 us (8%)
  between operations  13.8 us (2%)
  local copies, waits for them, and re-layouts  10.8 us (2%)
    unnamed x4, waiting for transfers between devices  188 us
    psum x1, waiting for transfers between devices, shards(): lax.psum((grads[0], grads[1], grads[2], grads[3], grads[4], grads[5]), ('...  187 us
    psum x1, blocking collectives, shards(): lax.psum((grads[0], grads[1], grads[2], grads[3], grads[4], grads[5]), ('...  79.9 us
    reduce_scatter x1, waiting for transfers between devices, shards(): lax.psum_scatter(lax.dot_general(grad_out, coef, (((0,), (0,)), ((), ()))...  68.8 us
    dot_general x1, matrix products, trunk_forward(): jnp.dot(points.T, w_first, precision=lax.Precision.HIGHEST, preferred_ele...  14.6 us
  transfers between devices with their start and end apart: 3, of which 3 were waited for; matrix products, arithmetic and copies ran while one was open for 7% of the time, Pallas kernels for 0%

commit v1 on v0

v1 whole, which is shorter than its diff:
```python
import jax
import jax.numpy as jnp
from jax import lax
from jax.experimental import pallas as pl
from jax.experimental.pallas import tpu as pltpu
from jax.sharding import Mesh, PartitionSpec as P

SPLIT = (("xh", 2), ("z", 8), ("xl", 2), ("y", 4), ("c", 2))
AXES = tuple(name for name, _ in SPLIT)
SIZES = tuple(size for _, size in SPLIT)
PLANE = ("xh", "xl", "y")
VMEM_BYTES = 48 * 1024 * 1024
BF16, F32 = jnp.bfloat16, jnp.float32


def nn(a, b):
    return lax.dot_general(a, b, (((1,), (0,)), ((), ())), preferred_element_type=F32)


def nt(a, b):
    return lax.dot_general(a, b, (((1,), (1,)), ((), ())), preferred_element_type=F32)


def tn(a, b):
    return lax.dot_general(a, b, (((0,), (0,)), ((), ())), preferred_element_type=F32)


def fold(a):
    return jnp.concatenate([a[:, :128], a[:, 128:]], axis=0)


def compute_kernel(
    place_ref, recv_ref, coords_ref, w_first_ref, b_first_ref, w_second_ref, b_second_ref,
    w_third_ref, b_third_ref, out_ref, one_ref, two_ref, grad_basis_ref, pre_two_ref, coef_ref,
):
    core, block = place_ref[0], place_ref[1]
    points = one_ref.shape[1]
    half = w_second_ref.shape[0] // 2
    own = pl.ds(pl.multiple_of(core * half, half), half)
    xyz = coords_ref[:, pl.ds(pl.multiple_of(block * points, points), points)]
    w_one = w_first_ref[...].T
    z_one = w_one[:, 0:1] * xyz[0:1] + w_one[:, 1:2] * xyz[1:2] + w_one[:, 2:3] * xyz[2:3]
    one_ref[...] = jnp.tanh(z_one + b_first_ref[...].T).astype(BF16)
    two_ref[...] = jnp.tanh(tn(w_second_ref[...], one_ref[...]) + b_second_ref[...].T).astype(BF16)
    basis = (tn(w_third_ref[...], two_ref[...]) + b_third_ref[...].T).astype(BF16)

    grads = recv_ref[:, :points]
    coef_ref[...] = nt(grads, basis)
    grad_basis_ref[...] = tn(recv_ref[:, points:], grads).astype(BF16)
    out_ref[:, :16, :512] = nt(two_ref[own, :], grad_basis_ref[...]).astype(BF16).reshape(16, 16, 512)
    two = two_ref[...].astype(F32)
    pre_two_ref[...] = (nn(w_third_ref[...], grad_basis_ref[...]) * (1.0 - two * two)).astype(BF16)
    out_ref[:, 16:, :512] = nt(one_ref[own, :], pre_two_ref[...]).astype(BF16).reshape(16, 16, 512)
    one = one_ref[own, :].astype(F32)
    pre_one = nn(w_second_ref[own, :], pre_two_ref[...]) * (1.0 - one * one)

    ones = jnp.ones((8, points), BF16)
    xyz_hi = xyz.astype(BF16)
    rest = xyz - xyz_hi.astype(F32)
    xyz_mid = rest.astype(BF16)
    xyz_lo = rest - xyz_mid.astype(F32)
    rows = jnp.concatenate(
        [xyz_hi.astype(F32), xyz_mid.astype(F32), xyz_lo, jnp.ones((7, points), F32)], axis=0
    ).astype(BF16)
    pre_hi = pre_one.astype(BF16)
    pre_rest = pre_one - pre_hi.astype(F32)
    pre_mid = pre_rest.astype(BF16)
    pre_lo = (pre_rest - pre_mid.astype(F32)).astype(BF16)
    terms = nt(rows, pre_hi) + nt(rows, pre_mid) + nt(rows, pre_lo)
    grad_w_first = terms[0:3] + terms[3:6] + terms[6:9]
    small = jnp.concatenate(
        [
            grad_w_first,
            terms[9:10],
            nt(ones, pre_two_ref[own, :])[0:1],
            nt(ones, grad_basis_ref[own, :])[0:1],
            jnp.zeros((2, half), F32),
        ],
        axis=0,
    )
    out_ref[0, 16:, 512:] = fold(small).astype(BF16)
    for at in range(16):
        if at:
            out_ref[at, 16:, 512:] = jnp.zeros((16, 128), BF16)
        group, column = at % 8, at // 8
        mine = coef_ref[pl.ds(pl.multiple_of(group * 16 + core * 8, 8), 8), column * half : column * half + half]
        out_ref[at, :16, 512:] = fold(mine).astype(BF16)


def finish_kernel(core_ref, own_ref, other_ref, w_first_ref, b_first_ref, w_second_ref, b_second_ref, w_third_ref, b_third_ref):
    half = 256
    for at, ref in ((core_ref[0], own_ref), (1 - core_ref[0], other_ref)):
        where = pl.ds(pl.multiple_of(at * half, half), half)
        w_third_ref[where, :] = ref[:, :16, :512].reshape(half, 512).astype(F32)
        w_second_ref[where, :] = ref[:, 16:, :512].reshape(half, 512).astype(F32)
        small = ref[0, 16:, 512:].astype(F32)
        small = jnp.concatenate([small[:8], small[8:]], axis=1)
        w_first_ref[:, where] = small[0:3]
        b_first_ref[:, where] = small[3:4]
        b_second_ref[:, where] = small[4:5]
        b_third_ref[:, where] = small[5:6]


def swap(value, flip):
    axis, bits = flip
    return lax.ppermute(value, axis, [(i, i ^ bits) for i in range(dict(SPLIT)[axis])])


def shards(grad_out, coef, coords, w_first, b_first, w_second, b_second, w_third, b_third):
    xl, y, core = lax.axis_index("xl"), lax.axis_index("y"), lax.axis_index("c")
    points = grad_out.shape[1] // 8
    smem = pl.BlockSpec(memory_space=pltpu.SMEM)
    vmem = pl.BlockSpec(memory_space=pltpu.VMEM)

    blocks = grad_out.reshape(8, 8, points).transpose(1, 0, 2)
    send = jnp.concatenate([blocks, jnp.broadcast_to(coef, (8, *coef.shape))], axis=2)
    send = jnp.broadcast_to(send[:, None], (8, 2, *send.shape[1:])).reshape(16, 8, points + 512)
    recv = lax.all_to_all(send, ("xl", "y", "c"), 0, 0, tiled=True).reshape(128, points + 512)

    place = jnp.stack([core, xl * 4 + y]).astype(jnp.int32)
    partial = pl.pallas_call(
        compute_kernel,
        out_shape=jax.ShapeDtypeStruct((16, 32, 640), BF16),
        in_specs=[smem] + [vmem] * 8,
        out_specs=vmem,
        scratch_shapes=[pltpu.VMEM((512, points), BF16)] * 4 + [pltpu.VMEM((128, 512), F32)],
        compiler_params=pltpu.CompilerParams(vmem_limit_bytes=VMEM_BYTES),
    )(place, recv, coords, w_first, b_first[None], w_second, b_second[None], w_third, b_third[None])

    parts = lax.all_to_all(partial, PLANE, 0, 0, tiled=True)
    mine = jnp.sum(parts.astype(F32), axis=0).astype(BF16)
    one, two, three = (swap(mine, ("z", bits)).astype(F32) for bits in (1, 2, 3))
    mine = ((mine.astype(F32) + one) + (two + three)).astype(BF16)
    mine = (mine.astype(F32) + swap(mine, ("z", 7)).astype(F32)).astype(BF16)

    gathered = lax.all_to_all(jnp.broadcast_to(mine, (16, 32, 640)), PLANE, 0, 0, tiled=True)
    other = swap(gathered, ("c", 1))
    own_coef = mine[:16, 512:].astype(F32)
    own_coef = jnp.concatenate([own_coef[:8], own_coef[8:]], axis=1)
    grad_coef = lax.dynamic_slice_in_dim(own_coef, lax.axis_index("z") * 32, 32, 1)

    row = jax.ShapeDtypeStruct((1, 512), F32)
    square = jax.ShapeDtypeStruct((512, 512), F32)
    w_one, b_one, w_two, b_two, w_three, b_three = pl.pallas_call(
        finish_kernel,
        out_shape=(jax.ShapeDtypeStruct((3, 512), F32), row, square, row, square, row),
        in_specs=[smem, vmem, vmem],
        out_specs=(vmem,) * 6,
        compiler_params=pltpu.CompilerParams(vmem_limit_bytes=VMEM_BYTES),
    )(place[:1], gathered, other)
    return (grad_coef, w_one, b_one[0], w_two, b_two[0], w_three, b_three[0])


def solution(mesh):
    fine = Mesh(mesh.devices.reshape(SIZES), AXES)
    fn, pts = ("xl", "y", "c"), ("xh", "z")
    return jax.shard_map(
        shards,
        mesh=fine,
        in_specs=(P(fn, pts), P(fn, None), P(None, pts), P(), P(), P(), P(), P(), P()),
        out_specs=(P(fn, pts), P(), P(), P(), P(), P(), P()),
        check_vma=False,
    )
```

time: 598 us -> 76.1 us (0.13)
  waiting for transfers between devices: 444 us -> 14.1 us
  blocking collectives: 79.9 us -> 30.1 us
  matrix products: 47.7 us -> 0 us
  starting transfers between devices: 0.3 us -> 20.1 us
  between operations: 13.8 us -> 0.72 us
  local copies, waits for them, and re-layouts: 10.8 us -> 2.21 us
  Pallas kernels: 0 us -> 6.72 us
    unnamed x4 -> x0, waiting for transfers between devices: 188 us -> none
    psum x1 -> x0, waiting for transfers between devices: 187 us -> none  [shards(): lax.psum((grads[0], grads[1], grads[2], grads[3], grads[4], grads[5]), ('...]
    psum x1 -> x0, blocking collectives: 79.9 us -> none  [shards(): lax.psum((grads[0], grads[1], grads[2], grads[3], grads[4], grads[5]), ('...]
    reduce_scatter x1 -> x0, waiting for transfers between devices: 68.8 us -> none  [shards(): lax.psum_scatter(lax.dot_general(grad_out, coef, (((0,), (0,)), ((), ()))...]
    dot_general x9 -> x0, matrix products: 47.7 us -> none  [the longest x1 14.6 us: trunk_forward(): jnp.dot(points.T, w_first, precision=lax.Precision.HIGHEST, preferred_ele...]
    all_to_all x0 -> x2, blocking collectives: none -> 30.1 us  [the longest x1 17.2 us: shards(): parts = lax.all_to_all(partial, PLANE, 0, 0, tiled=True)]
    ppermute x0 -> x5, starting transfers between devices: none -> 13.1 us  [swap(): lax.ppermute(value, axis, [(i, i ^ bits) for i in range(dict(SPLIT)[axis])])]
    unnamed x24 -> x14, local copies, waits for them, and re-layouts: 10.8 us -> 0.68 us
  transfers between devices with their start and end apart: 3 -> 6, of which waited for: 3 -> 5; matrix products, arithmetic and copies ran while one was open for 7% -> 1% of each run, Pallas kernels for 0% -> 0%
where the time goes in v1:
time: 76.1 us; the launch traced here: 75.7 us
  blocking collectives  30.1 us (40%)
  starting transfers between devices  20.1 us (26%)
  waiting for transfers between devices  14.1 us (19%)
  Pallas kernels  6.72 us (9%)
  local copies, waits for them, and re-layouts  2.21 us (3%)
  other arithmetic  1.8 us (2%)
    all_to_all x1, blocking collectives, shards(): parts = lax.all_to_all(partial, PLANE, 0, 0, tiled=True)  17.2 us
    ppermute x5, starting transfers between devices, swap(): lax.ppermute(value, axis, [(i, i ^ bits) for i in range(dict(SPLIT)[axis])])  13.1 us
    all_to_all x1, blocking collectives, shards(): lax.all_to_all(jnp.broadcast_to(mine, (16, 32, 640)), PLANE, 0, 0, tiled=...  12.9 us
    all_to_all x1, waiting for transfers between devices, shards(): lax.all_to_all(send, ('xl', 'y', 'c'), 0, 0, tiled=True)  8.29 us
    all_to_all x1, starting transfers between devices, shards(): lax.all_to_all(send, ('xl', 'y', 'c'), 0, 0, tiled=True)  7.05 us
    ppermute x5, waiting for transfers between devices, swap(): lax.ppermute(value, axis, [(i, i ^ bits) for i in range(dict(SPLIT)[axis])])  5.81 us
    pallas_call x1, Pallas kernels, shards(): pl.pallas_call(compute_kernel, out_shape=jax.ShapeDtypeStruct((16, 32, 64...  5.3 us
  transfers between devices with their start and end apart: 6, of which 5 were waited for; matrix products, arithmetic and copies ran while one was open for 1% of the time, Pallas kernels for 0%

profile of v1, /device:TPU:1, one launch (start us, length us, event | category | flops | bytes accessed | tf_op | source)
XLA Modules:
  0.0 75.7 jit_solution(14679503047649610897)
XLA Ops:
  0.6 0.7 broadcast_in_dim.21
  1.3 0.9 %pad_maximum_fusion = bf16[8,8,1536]{2,1,0:T(8,128)(2,1)S(1)} fusion(bf16[8,8,512]{2,1,0:T(8,128)(2,1)S(1)} %broadcast_in_dim.21, bf16[8,8,1024]{2,1,0:T(8,128)(2,1)} %bitcast.17), kind=kLoop, calls=%fused_computation | loop fusion | flops 393216 | bytes 393216 | tf_op jit(solution)/shard_map/concatenate | solution.py:116
  2.3 0.0 copy-start.1
  2.3 0.8 %broadcast_in_dim.22 = bf16[8,2,8,1536]{3,2,1,0:T(8,128)(2,1)} broadcast(bf16[8,8,1536]{2,1,0:T(8,128)(2,1)S(1)} %pad_maximum_fusion), dimensions={0,2,3} | broadcast | bytes 589824 | tf_op jit(solution)/shard_map/broadcast_in_dim | solution.py:117
  3.0 7.0 %all-to-all-start = ((bf16[16,8,1536]{2,1,0:T(8,128)(2,1)}), bf16[16,8,1536]{2,1,0:T(8,128)(2,1)S(1)}, u32[]{:S(2)}, u32[]{:S(2)}) async-start(bf16[16,8,1536]{2,1,0:T(8,128)(2,1)} %bitcast.4), calls=%async_computation | async-start | bytes 786432 | tf_op jit(solution)/shard_map/all_to_all | solution.py:118
  10.1 0.0 copy-start.3
  10.1 0.1 pad_add_fusion.place_ref
  10.2 8.3 %all-to-all-done = bf16[16,8,1536]{2,1,0:T(8,128)(2,1)S(1)} async-done(((bf16[16,8,1536]{2,1,0:T(8,128)(2,1)}), bf16[16,8,1536]{2,1,0:T(8,128)(2,1)S(1)}, u32[]{:S(2)}, u32[]{:S(2)}) %all-to-all-start) | async-done | bytes 393248 | tf_op jit(solution)/shard_map/all_to_all | solution.py:118
  18.5 0.0 copy-done.1
  18.5 0.0 copy-done
  18.5 0.0 copy-done.2
  18.5 0.0 copy-done.6
  18.5 0.0 copy-done.3
  18.5 0.6 copy-done.5
  19.2 0.0 copy-done.4
  19.2 5.3 %shard_map.144 = bf16[16,32,640]{2,1,0:T(8,128)(2,1)S(1)} custom-call(s32[2]{0:T(128)S(1)} %pad_add_fusion.place_ref, bf16[128,1536]{1,0:T(8,128)(2,1)S(1)} %bitcast.13, f32[3,8192]{1,0:T(4,128)S(1)} %copy-done.2, f32[3,512]{1,0:T(4,128)S(1)} %copy-done.3, f32[1,512]{1,0:T(1,128)S(1)} %bitcast.14, bf16[512,512]{1,0:T(8,128)(2,1)S(1)} %copy-done, ...), custom_call_target="tpu_custom_call" | custom-call | tf_op jit(solution)/shard_map/pallas_call | solution.py:121
  24.5 17.2 %all_to_all.15 = bf16[16,32,640]{2,1,0:T(8,128)(2,1)S(1)} all-to-all(bf16[16,32,640]{2,1,0:T(8,128)(2,1)S(1)} %shard_map.144), channel_id=1, replica_groups=mesh['xh'=2,'z'=8,'xl'=2,'y'=4,'c'=2] {'xh','xl','y'}, dimensions={0} | all-to-all | bytes 1310720 | tf_op jit(solution)/shard_map/all_to_all | solution.py:130
  41.7 0.1 reduce_sum.12
  41.8 4.4 %collective-permute-start.2 = (bf16[32,640]{1,0:T(8,128)(2,1)S(1)}, bf16[32,640]{1,0:T(8,128)(2,1)S(1)}, u32[]{:S(2)}, u32[]{:S(2)}) collective-permute-start(bf16[32,640]{1,0:T(8,128)(2,1)S(1)} %reduce_sum.12), channel_id=1, source_target_pairs={{0,48},{16,32},{32,16},{48,0},{64,112},{80,96},{96,80},{112,64},{1... | collective-permute-start | bytes 122888 | tf_op jit(solution)/shard_map/ppermute | solution.py:106
  46.2 0.0 collective-permute-start.1
  46.2 0.4 collective-permute-start
  46.6 1.0 %collective-permute-done.2 = bf16[32,640]{1,0:T(8,128)(2,1)S(1)} collective-permute-done((bf16[32,640]{1,0:T(8,128)(2,1)S(1)}, bf16[32,640]{1,0:T(8,128)(2,1)S(1)}, u32[]{:S(2)}, u32[]{:S(2)}) %collective-permute-start.2) | collective-permute-done | bytes 40992 | tf_op jit(solution)/shard_map/ppermute | solution.py:106
  47.6 2.4 %collective-permute-done.1 = bf16[32,640]{1,0:T(8,128)(2,1)S(1)} collective-permute-done((bf16[32,640]{1,0:T(8,128)(2,1)S(1)}, bf16[32,640]{1,0:T(8,128)(2,1)S(1)}, u32[]{:S(2)}, u32[]{:S(2)}) %collective-permute-start.1) | collective-permute-done | bytes 40992 | tf_op jit(solution)/shard_map/ppermute | solution.py:106
  49.9 0.0 collective-permute-done
  50.0 3.5 %collective-permute-start.3 = (bf16[32,640]{1,0:T(8,128)(2,1)S(1)}, bf16[32,640]{1,0:T(8,128)(2,1)S(1)}, u32[]{:S(2)}, u32[]{:S(2)}) collective-permute-start(bf16[32,640]{1,0:T(8,128)(2,1)S(1)} %add_convert_fusion.1), channel_id=1, source_target_pairs={{0,112},{16,96},{32,80},{48,64},{64,48},{80,32},{96,16},{112,0},{1... | collective-permute-start | bytes 122888 | tf_op jit(solution)/shard_map/ppermute | solution.py:106
  53.5 1.4 %collective-permute-done.3 = bf16[32,640]{1,0:T(8,128)(2,1)S(1)} collective-permute-done((bf16[32,640]{1,0:T(8,128)(2,1)S(1)}, bf16[32,640]{1,0:T(8,128)(2,1)S(1)}, u32[]{:S(2)}, u32[]{:S(2)}) %collective-permute-start.3) | collective-permute-done | bytes 40992 | tf_op jit(solution)/shard_map/ppermute | solution.py:106
  54.9 0.1 broadcast_in_dim.26
  55.0 12.9 %all_to_all.16.own_ref = bf16[16,32,640]{2,1,0:T(8,128)(2,1)S(1)} all-to-all(bf16[16,32,640]{2,1,0:T(8,128)(2,1)S(1)} %broadcast_in_dim.26), channel_id=1, replica_groups=mesh['xh'=2,'z'=8,'xl'=2,'y'=4,'c'=2] {'xh','xl','y'}, dimensions={0} | all-to-all | bytes 1310720 | tf_op jit(solution)/shard_map/all_to_all | solution.py:136
  67.9 4.7 %collective-permute-start.4 = (bf16[16,32,640]{2,1,0:T(8,128)(2,1)S(1)}, bf16[16,32,640]{2,1,0:T(8,128)(2,1)S(1)}, u32[]{:S(2)}, u32[]{:S(2)}) collective-permute-start(bf16[16,32,640]{2,1,0:T(8,128)(2,1)S(1)} %all_to_all.16.own_ref), channel_id=1, source_target_pairs={{0,1},{1,0},{2,3},{3,2},{4,5},{5,4},{6,7},{7,6},{8,9},{9,8},{10,11... | collective-permute-start | bytes 1966088 | tf_op jit(solution)/shard_map/ppermute | solution.py:106
  72.6 0.7 fusion
  73.3 1.0 %collective-permute-done.4.other_ref = bf16[16,32,640]{2,1,0:T(8,128)(2,1)S(1)} collective-permute-done((bf16[16,32,640]{2,1,0:T(8,128)(2,1)S(1)}, bf16[16,32,640]{2,1,0:T(8,128)(2,1)S(1)}, u32[]{:S(2)}, u32[]{:S(2)}) %collective-permute-start.4) | collective-permute-done | bytes 655392 | tf_op jit(solution)/shard_map/ppermute | solution.py:106
  74.3 1.4 %shard_map.145 = (f32[3,512]{1,0:T(4,128)}, f32[1,512]{1,0:T(1,128)}, f32[512,512]{1,0:T(8,128)}, f32[1,512]{1,0:T(1,128)}, f32[512,512]{1,0:T(8,128)}, /*index=5*/f32[1,512]{1,0:T(1,128)}) custom-call(s32[1]{0:T(128)} %bitcast.core_ref, bf16[16,32,640]{2,1,0:T(8,128)(2,1)S(1)} %all_to_all.16.own_ref, bf16[16,32,640]{2,1,0:T(8,128)(2,1)S(1)} %collective-permute-done.4.other_ref), custom_call_target="tpu_custom_call" | custom-call | tf_op jit(solution)/shard_map/pallas_call | solution.py:144
  (9 shorter events, 0.1 us)
Async XLA Ops:
  2.3 16.2 %copy-start.1 = (bf16[512,512]{1,0:T(8,128)(2,1)S(1)}, bf16[512,512]{1,0:T(8,128)(2,1)}, u32[]{:S(2)}) copy-start(bf16[512,512]{1,0:T(8,128)(2,1)} %w_third_ref.1) | copy-start | bytes 1572868
  3.0 15.4 %copy-start = (bf16[512,512]{1,0:T(8,128)(2,1)S(1)}, bf16[512,512]{1,0:T(8,128)(2,1)}, u32[]{:S(2)}) copy-start(bf16[512,512]{1,0:T(8,128)(2,1)} %w_second_ref.1) | copy-start | bytes 1572868
  3.0 15.5 %copy-start.2 = (f32[3,8192]{1,0:T(4,128)S(1)}, f32[3,8192]{1,0:T(4,128)}, u32[]{:S(2)}) copy-start(f32[3,8192]{1,0:T(4,128)} %coords_ref.1) | copy-start | bytes 294916
  3.0 15.4 %all-to-all-start = ((bf16[16,8,1536]{2,1,0:T(8,128)(2,1)}), bf16[16,8,1536]{2,1,0:T(8,128)(2,1)S(1)}, u32[]{:S(2)}, u32[]{:S(2)}) async-start(bf16[16,8,1536]{2,1,0:T(8,128)(2,1)} %bitcast.4), calls=%async_computation | async-start | bytes 786432 | tf_op jit(solution)/shard_map/all_to_all | solution.py:118
  10.1 8.4 %copy-start.6 = (f32[512]{0:T(512)S(1)}, f32[512]{0:T(512)}, u32[]{:S(2)}) copy-start(f32[512]{0:T(512)} %param.17) | copy-start | bytes 6148
  10.1 8.4 %copy-start.3 = (f32[3,512]{1,0:T(4,128)S(1)}, f32[3,512]{1,0:T(4,128)}, u32[]{:S(2)}) copy-start(f32[3,512]{1,0:T(4,128)} %w_first_ref.1) | copy-start | bytes 18436
  18.5 0.7 copy-start.5
  18.5 0.7 copy-start.4
  41.8 5.8 %collective-permute-start.2 = (bf16[32,640]{1,0:T(8,128)(2,1)S(1)}, bf16[32,640]{1,0:T(8,128)(2,1)S(1)}, u32[]{:S(2)}, u32[]{:S(2)}) collective-permute-start(bf16[32,640]{1,0:T(8,128)(2,1)S(1)} %reduce_sum.12), channel_id=1, source_target_pairs={{0,48},{16,32},{32,16},{48,0},{64,112},{80,96},{96,80},{112,64},{1... | collective-permute-start | bytes 122888 | tf_op jit(solution)/shard_map/ppermute | solution.py:106
  46.2 3.8 %collective-permute-start.1 = (bf16[32,640]{1,0:T(8,128)(2,1)S(1)}, bf16[32,640]{1,0:T(8,128)(2,1)S(1)}, u32[]{:S(2)}, u32[]{:S(2)}) collective-permute-start(bf16[32,640]{1,0:T(8,128)(2,1)S(1)} %reduce_sum.12), channel_id=1, source_target_pairs={{0,32},{16,48},{32,0},{48,16},{64,96},{80,112},{96,64},{112,80},{1... | collective-permute-start | bytes 122888 | tf_op jit(solution)/shard_map/ppermute | solution.py:106
  46.2 3.8 %collective-permute-start = (bf16[32,640]{1,0:T(8,128)(2,1)S(1)}, bf16[32,640]{1,0:T(8,128)(2,1)S(1)}, u32[]{:S(2)}, u32[]{:S(2)}) collective-permute-start(bf16[32,640]{1,0:T(8,128)(2,1)S(1)} %reduce_sum.12), channel_id=1, source_target_pairs={{0,16},{16,0},{32,48},{48,32},{64,80},{80,64},{96,112},{112,96},{1... | collective-permute-start | bytes 122888 | tf_op jit(solution)/shard_map/ppermute | solution.py:106
  50.0 4.9 %collective-permute-start.3 = (bf16[32,640]{1,0:T(8,128)(2,1)S(1)}, bf16[32,640]{1,0:T(8,128)(2,1)S(1)}, u32[]{:S(2)}, u32[]{:S(2)}) collective-permute-start(bf16[32,640]{1,0:T(8,128)(2,1)S(1)} %add_convert_fusion.1), channel_id=1, source_target_pairs={{0,112},{16,96},{32,80},{48,64},{64,48},{80,32},{96,16},{112,0},{1... | collective-permute-start | bytes 122888 | tf_op jit(solution)/shard_map/ppermute | solution.py:106
  67.9 6.4 %collective-permute-start.4 = (bf16[16,32,640]{2,1,0:T(8,128)(2,1)S(1)}, bf16[16,32,640]{2,1,0:T(8,128)(2,1)S(1)}, u32[]{:S(2)}, u32[]{:S(2)}) collective-permute-start(bf16[16,32,640]{2,1,0:T(8,128)(2,1)S(1)} %all_to_all.16.own_ref), channel_id=1, source_target_pairs={{0,1},{1,0},{2,3},{3,2},{4,5},{5,4},{6,7},{7,6},{8,9},{9,8},{10,11... | collective-permute-start | bytes 1966088 | tf_op jit(solution)/shard_map/ppermute | solution.py:106

commit v2 on v1

v2 whole, which is shorter than its diff:
```python
import jax
import jax.numpy as jnp
from jax import lax
from jax.experimental import pallas as pl
from jax.experimental.pallas import tpu as pltpu
from jax.sharding import Mesh, PartitionSpec as P

SPLIT = (("xh", 2), ("z", 8), ("xl", 2), ("y", 4), ("c", 2))
AXES = tuple(name for name, _ in SPLIT)
SIZES = tuple(size for _, size in SPLIT)
PLANE = ("xh", "xl", "y")
VMEM_BYTES = 20 * 1024 * 1024
BF16, F32 = jnp.bfloat16, jnp.float32


def nn(a, b):
    return lax.dot_general(a, b, (((1,), (0,)), ((), ())), preferred_element_type=F32)


def nt(a, b):
    return lax.dot_general(a, b, (((1,), (1,)), ((), ())), preferred_element_type=F32)


def tn(a, b):
    return lax.dot_general(a, b, (((0,), (0,)), ((), ())), preferred_element_type=F32)


def fold(a):
    return jnp.concatenate([a[:, :128], a[:, 128:]], axis=0)


def across(a):
    total = a[:, :128]
    for at in range(128, a.shape[1], 128):
        total = total + a[:, at : at + 128]
    return jnp.sum(total.T, axis=0, keepdims=True)


def unfold(a):
    return jnp.concatenate([a[:8], a[8:]], axis=1)


def pack_kernel(grad_out_ref, coef_ref, out_ref):
    blocks, rows, width = out_ref.shape
    points = width - coef_ref.shape[1]
    for at in range(blocks):
        out_ref[at, :, :points] = grad_out_ref[:, at * points : (at + 1) * points]
        out_ref[at, :, points:] = coef_ref[...]


def forward_kernel(
    coords_ref, w_first_ref, b_first_ref, w_second_ref, b_second_ref, w_third_ref, b_third_ref,
    acts_ref, basis_ref, xyz_ref, small_ref, bias_ref, weights_ref, sems,
):
    one_ref, two_ref = acts_ref.at[0], acts_ref.at[1]
    points = one_ref.shape[1]
    at = lax.axis_index("xl") * 4 + lax.axis_index("y")
    block = pl.ds(pl.multiple_of(at * points, points), points)
    copies = [
        pltpu.make_async_copy(coords_ref.at[:, block], xyz_ref, sems.at[0]),
        pltpu.make_async_copy(w_first_ref, small_ref, sems.at[1]),
        pltpu.make_async_copy(b_first_ref, bias_ref.at[0], sems.at[2]),
        pltpu.make_async_copy(b_second_ref, bias_ref.at[1], sems.at[3]),
        pltpu.make_async_copy(b_third_ref, bias_ref.at[2], sems.at[4]),
        pltpu.make_async_copy(w_second_ref, weights_ref.at[0], sems.at[5]),
        pltpu.make_async_copy(w_third_ref, weights_ref.at[1], sems.at[6]),
    ]
    for copy in copies:
        copy.start()
    for copy in copies[:5]:
        copy.wait()
    xyz = xyz_ref[...]
    w_one = small_ref[...].T
    z_one = w_one[:, 0:1] * xyz[0:1] + w_one[:, 1:2] * xyz[1:2] + w_one[:, 2:3] * xyz[2:3]
    one_ref[...] = jnp.tanh(z_one + bias_ref[0].T).astype(BF16)
    copies[5].wait()
    two_ref[...] = jnp.tanh(tn(weights_ref[0], one_ref[...]) + bias_ref[1].T).astype(BF16)
    copies[6].wait()
    basis_ref[...] = (tn(weights_ref[1], two_ref[...]) + bias_ref[2].T).astype(BF16)


def middle_kernel(near_ref, basis_ref, w_second_ref, w_third_ref, coef_ref, weights_ref, sems):
    copies = [
        pltpu.make_async_copy(w_second_ref, weights_ref.at[0], sems.at[0]),
        pltpu.make_async_copy(w_third_ref, weights_ref.at[1], sems.at[1]),
    ]
    for copy in copies:
        copy.start()
    coef_ref[...] = nt(near_ref[:, : basis_ref.shape[1]], basis_ref[...])
    for copy in copies:
        copy.wait()


def backward_kernel(
    near_ref, far_ref, xyz_ref, weights_ref, coef_ref, acts_ref, out_ref, grad_basis_ref, pre_two_ref
):
    one_ref, two_ref = acts_ref.at[0], acts_ref.at[1]
    w_second_ref, w_third_ref = weights_ref.at[0], weights_ref.at[1]
    core = lax.axis_index("c")
    points = one_ref.shape[1]
    half = w_second_ref.shape[0] // 2
    own = pl.ds(pl.multiple_of(core * half, half), half)
    grad_basis = tn(near_ref[:, points:], near_ref[:, :points])
    grad_basis = grad_basis + tn(far_ref[:, points:], far_ref[:, :points])
    grad_basis_ref[...] = grad_basis.astype(BF16)
    out_ref[:, :16, :512] = nt(two_ref[own, :], grad_basis_ref[...]).astype(BF16).reshape(16, 16, 512)
    two = two_ref[...].astype(F32)
    pre_two_ref[...] = (nn(w_third_ref[...], grad_basis_ref[...]) * (1.0 - two * two)).astype(BF16)
    out_ref[:, 16:, :512] = nt(one_ref[own, :], pre_two_ref[...]).astype(BF16).reshape(16, 16, 512)
    one = one_ref[own, :].astype(F32)
    pre_one = nn(w_second_ref[own, :], pre_two_ref[...]) * (1.0 - one * one)

    xyz = xyz_ref[...]
    small = [across(pre_one * xyz[axis : axis + 1]) for axis in range(3)]
    small += [across(pre_one), across(pre_two_ref[own, :].astype(F32))]
    small += [across(grad_basis_ref[own, :].astype(F32)), jnp.zeros((2, half), F32)]
    small = fold(jnp.concatenate(small, axis=0)).astype(BF16)
    for at in range(16):
        group, column = at % 8, at // 8
        mine = coef_ref[group * 8 : group * 8 + 8, column * half : column * half + half]
        out_ref[at, :16, 512:] = fold(mine).astype(BF16)
        out_ref[at, 16:, 512:] = small


def finish_kernel(
    own_ref, other_ref, own_small_ref, other_small_ref, w_first_ref, b_first_ref, w_second_ref,
    b_second_ref, w_third_ref, b_third_ref,
):
    core, half = lax.axis_index("c"), 256
    for at, ref, small_ref in ((core, own_ref, own_small_ref), (1 - core, other_ref, other_small_ref)):
        where = pl.ds(pl.multiple_of(at * half, half), half)
        w_third_ref[where, :] = ref[:, :16, :].reshape(half, 512).astype(F32)
        w_second_ref[where, :] = ref[:, 16:, :].reshape(half, 512).astype(F32)
        small = unfold(small_ref[...].astype(F32))
        w_first_ref[:, where] = small[0:3]
        b_first_ref[:, where] = small[3:4]
        b_second_ref[:, where] = small[4:5]
        b_third_ref[:, where] = small[5:6]


def swap(value, flip):
    axis, bits = flip
    return lax.ppermute(value, axis, [(i, i ^ bits) for i in range(dict(SPLIT)[axis])])


def shards(grad_out, coef, coords, w_first, b_first, w_second, b_second, w_third, b_third):
    points = grad_out.shape[1] // 8
    vmem = pl.BlockSpec(memory_space=pltpu.VMEM)
    hbm = pl.BlockSpec(memory_space=pltpu.HBM)

    coords, w_first, b_first, w_second, b_second, w_third, b_third = (
        pltpu.with_memory_space_constraint(value, pltpu.HBM)
        for value in (coords, w_first, b_first[None], w_second, b_second[None], w_third, b_third[None])
    )
    send = pl.pallas_call(
        pack_kernel,
        out_shape=pltpu.VMEM((8, 8, points + 512), BF16),
        in_specs=[vmem, vmem],
        out_specs=vmem,
    )(grad_out, coef)
    near = lax.all_to_all(send, ("xl", "y"), 0, 0, tiled=True).reshape(64, points + 512)
    acts, basis, xyz = pl.pallas_call(
        forward_kernel,
        out_shape=(
            pltpu.VMEM((2, 512, points), BF16),
            pltpu.VMEM((512, points), BF16),
            pltpu.VMEM((3, points), F32),
        ),
        in_specs=[hbm] * 7,
        out_specs=(vmem,) * 3,
        scratch_shapes=[
            pltpu.VMEM((3, 512), F32),
            pltpu.VMEM((3, 1, 512), F32),
            pltpu.VMEM((2, 512, 512), BF16),
            pltpu.SemaphoreType.DMA((7,)),
        ],
        compiler_params=pltpu.CompilerParams(vmem_limit_bytes=VMEM_BYTES),
        cost_estimate=pl.CostEstimate(flops=2**30, bytes_accessed=5 * 2**20, transcendentals=2**20),
    )(coords, w_first, b_first, w_second, b_second, w_third, b_third)
    near, acts = lax.optimization_barrier((near, acts))
    far = swap(near, ("c", 1))
    coef_part, weights = pl.pallas_call(
        middle_kernel,
        out_shape=(pltpu.VMEM((64, 512), F32), pltpu.VMEM((2, 512, 512), BF16)),
        in_specs=[vmem, vmem, hbm, hbm],
        out_specs=(vmem,) * 2,
        scratch_shapes=[pltpu.SemaphoreType.DMA((2,))],
        compiler_params=pltpu.CompilerParams(vmem_limit_bytes=VMEM_BYTES),
        cost_estimate=pl.CostEstimate(flops=2**28, bytes_accessed=2 * 2**20, transcendentals=0),
    )(near, basis, w_second, w_third)
    partial = pl.pallas_call(
        backward_kernel,
        out_shape=jax.ShapeDtypeStruct((16, 32, 640), BF16),
        in_specs=[vmem] * 6,
        out_specs=vmem,
        scratch_shapes=[pltpu.VMEM((512, points), BF16)] * 2,
        compiler_params=pltpu.CompilerParams(vmem_limit_bytes=VMEM_BYTES),
        cost_estimate=pl.CostEstimate(flops=2**31, bytes_accessed=5 * 2**20, transcendentals=0),
    )(near, far, xyz, weights, coef_part, acts)

    parts = lax.all_to_all(partial, PLANE, 0, 0, tiled=True)
    mine = jnp.sum(parts.astype(F32), axis=0).astype(BF16)
    one, two, three = (swap(mine, ("z", bits)).astype(F32) for bits in (1, 2, 3))
    mine = ((mine.astype(F32) + one) + (two + three)).astype(BF16)
    mine = (mine.astype(F32) + swap(mine, ("z", 6)).astype(F32)).astype(BF16)

    small = mine[16:, 512:]
    other_small = swap(small, ("c", 1))
    gathered = jnp.broadcast_to(mine[:, :512], (16, 32, 512))
    gathered = lax.all_to_all(gathered, PLANE, 0, 0, tiled=True)
    other = swap(gathered, ("c", 1))
    row = jax.ShapeDtypeStruct((1, 512), F32)
    square = jax.ShapeDtypeStruct((512, 512), F32)
    z = lax.axis_index("z")
    grad_coef = lax.dynamic_slice(mine, (z // 4 * 8, 512 + z % 4 * 32), (8, 32)).astype(F32)
    w_one, b_one, w_two, b_two, w_three, b_three = pl.pallas_call(
        finish_kernel,
        out_shape=(jax.ShapeDtypeStruct((3, 512), F32), row, square, row, square, row),
        in_specs=[vmem] * 4,
        out_specs=(vmem,) * 6,
        compiler_params=pltpu.CompilerParams(vmem_limit_bytes=VMEM_BYTES),
    )(gathered, other, small, other_small)
    return (grad_coef, w_one, b_one[0], w_two, b_two[0], w_three, b_three[0])


def solution(mesh):
    fine = Mesh(mesh.devices.reshape(SIZES), AXES)
    fn, pts = ("xl", "y", "c"), ("xh", "z")
    return jax.shard_map(
        shards,
        mesh=fine,
        in_specs=(P(fn, pts), P(fn, None), P(None, pts), P(), P(), P(), P(), P(), P()),
        out_specs=(P(fn, pts), P(), P(), P(), P(), P(), P()),
        check_vma=False,
    )
```

time: 76.1 us -> 71.8 us (0.943)
  Pallas kernels: 6.72 us -> 10.1 us
  waiting for transfers between devices: 14.1 us -> 11.6 us
  local copies, waits for them, and re-layouts: 2.21 us -> 0.05 us
  blocking collectives: 30.1 us -> 28.3 us
  other arithmetic: 1.8 us -> 0.8 us
    all_to_all x1, waiting for transfers between devices: 8.29 us -> 2.5 us  [shards(): lax.all_to_all(send, ('xl', 'y'), 0, 0, tiled=True)]
    pallas_call x1 -> x4, Pallas kernels: 5.3 us -> 8.68 us  [the longest x1 3.37 us: shards(): pl.pallas_call(forward_kernel, out_shape=(pltpu.VMEM((2, 512, points), BF...]
    ppermute x5 -> x7, waiting for transfers between devices: 5.81 us -> 9.08 us  [swap(): lax.ppermute(value, axis, [(i, i ^ bits) for i in range(dict(SPLIT)[axis])])]
    concatenate x2 -> x0, other arithmetic: 1.58 us -> none  [the longest x1 0.92 us: shards(): jnp.concatenate([blocks, jnp.broadcast_to(coef, (8, *coef.shape))], axis=2)]
    broadcast_in_dim x3 -> x1, local copies, waits for them, and re-layouts: 1.53 us -> 0.04 us  [shards(): gathered = jnp.broadcast_to(mine[:, :512], (16, 32, 512))]
    all_to_all x1, starting transfers between devices: 7.05 us -> 5.95 us  [shards(): lax.all_to_all(send, ('xl', 'y'), 0, 0, tiled=True)]
    all_to_all x1, blocking collectives: 17.2 us -> 16.2 us  [shards(): parts = lax.all_to_all(partial, PLANE, 0, 0, tiled=True)]
    ppermute x5 -> x7, starting transfers between devices: 13.1 us -> 14 us  [swap(): lax.ppermute(value, axis, [(i, i ^ bits) for i in range(dict(SPLIT)[axis])])]
  transfers between devices with their start and end apart: 6 -> 8, of which waited for: 5 -> 5; matrix products, arithmetic and copies ran while one was open for 1% -> 1% of each run, Pallas kernels for 0% -> 6%
where the time goes in v2:
time: 71.8 us; the launch traced here: 71.5 us
  blocking collectives  28.3 us (39%)
  starting transfers between devices  20 us (28%)
  waiting for transfers between devices  11.6 us (16%)
  Pallas kernels  10.1 us (14%)
  other arithmetic  0.8 us (1%)
    all_to_all x1, blocking collectives, shards(): parts = lax.all_to_all(partial, PLANE, 0, 0, tiled=True)  16.2 us
    ppermute x7, starting transfers between devices, swap(): lax.ppermute(value, axis, [(i, i ^ bits) for i in range(dict(SPLIT)[axis])])  14 us
    all_to_all x1, blocking collectives, shards(): gathered = lax.all_to_all(gathered, PLANE, 0, 0, tiled=True)  12.1 us
    ppermute x7, waiting for transfers between devices, swap(): lax.ppermute(value, axis, [(i, i ^ bits) for i in range(dict(SPLIT)[axis])])  9.08 us
    all_to_all x1, starting transfers between devices, shards(): lax.all_to_all(send, ('xl', 'y'), 0, 0, tiled=True)  5.95 us
    pallas_call x1, Pallas kernels, shards(): pl.pallas_call(forward_kernel, out_shape=(pltpu.VMEM((2, 512, points), BF...  3.37 us
    all_to_all x1, waiting for transfers between devices, shards(): lax.all_to_all(send, ('xl', 'y'), 0, 0, tiled=True)  2.5 us
    pallas_call x1, Pallas kernels, shards(): pl.pallas_call(backward_kernel, out_shape=jax.ShapeDtypeStruct((16, 32, 6...  2.49 us
  transfers between devices with their start and end apart: 8, of which 5 were waited for; matrix products, arithmetic and copies ran while one was open for 1% of the time, Pallas kernels for 6%

profile of v2, /device:TPU:1, one launch (start us, length us, event | category | flops | bytes accessed | tf_op | source)
XLA Modules:
  0.0 71.5 jit_solution(9344789973307231580)
XLA Ops:
  0.6 1.6 %shard_map.144 = bf16[8,8,1536]{2,1,0:T(8,128)(2,1)} custom-call(bf16[8,8192]{1,0:T(8,128)(2,1)} %grad_out_ref.1, bf16[8,512]{1,0:T(8,128)(2,1)} %coef_ref.1), custom_call_target="tpu_custom_call" | custom-call | tf_op jit(solution)/shard_map/pallas_call | solution.py:155
  2.2 5.9 %all-to-all-start = ((bf16[8,8,1536]{2,1,0:T(8,128)(2,1)}), bf16[8,8,1536]{2,1,0:T(8,128)(2,1)S(1)}, u32[]{:S(2)}, u32[]{:S(2)}) async-start(bf16[8,8,1536]{2,1,0:T(8,128)(2,1)} %shard_map.144), calls=%async_computation | async-start | bytes 393216 | tf_op jit(solution)/shard_map/all_to_all | solution.py:161
  8.2 3.4 %shard_map.145 = (bf16[2,512,1024]{2,1,0:T(8,128)(2,1)S(1)}, bf16[512,1024]{1,0:T(8,128)(2,1)S(1)}, f32[3,1024]{1,0:T(4,128)S(1)}) custom-call(f32[3,8192]{1,0:T(4,128)} %coords_ref.1, f32[3,512]{1,0:T(4,128)} %w_first_ref.1, f32[1,512]{1,0:T(1,128)} %bitcast.10, bf16[512,512]{1,0:T(8,128)(2,1)} %w_second_ref.3, f32[1,512]{1,0:T(1,128)} %bitcast.11, ...), custom_call_target="tpu_custom_call" | custom-call | flops 1073741824 | bytes 5242880 | tf_op jit(solution)/shard_map/pallas_call | solution.py:162
  11.6 2.5 %all-to-all-done = bf16[8,8,1536]{2,1,0:T(8,128)(2,1)S(1)} async-done(((bf16[8,8,1536]{2,1,0:T(8,128)(2,1)}), bf16[8,8,1536]{2,1,0:T(8,128)(2,1)S(1)}, u32[]{:S(2)}, u32[]{:S(2)}) %all-to-all-start) | async-done | bytes 196640 | tf_op jit(solution)/shard_map/all_to_all | solution.py:161
  14.1 2.0 %collective-permute-start = (bf16[64,1536]{1,0:T(8,128)(2,1)S(1)}, bf16[64,1536]{1,0:T(8,128)(2,1)S(1)}, u32[]{:S(2)}, u32[]{:S(2)}) collective-permute-start(bf16[64,1536]{1,0:T(8,128)(2,1)S(1)} %bitcast.7), channel_id=1, source_target_pairs={{0,1},{1,0},{2,3},{3,2},{4,5},{5,4},{6,7},{7,6},{8,9},{9,8},{10,11... | collective-permute-start | bytes 589832 | tf_op jit(solution)/shard_map/ppermute | solution.py:143
  16.1 1.2 %shard_map.146 = (f32[64,512]{1,0:T(8,128)S(1)}, bf16[2,512,512]{2,1,0:T(8,128)(2,1)S(1)}) custom-call(bf16[64,1536]{1,0:T(8,128)(2,1)S(1)} %bitcast.8, bf16[512,1024]{1,0:T(8,128)(2,1)S(1)} %get-tuple-element.23.basis_ref, bf16[512,512]{1,0:T(8,128)(2,1)} %w_second_ref.3, bf16[512,512]{1,0:T(8,128)(2,1)} %w_third_ref.3), custom_call_target="tpu_custom_call" | custom-call | flops 268435456 | bytes 2097152 | tf_op jit(solution)/shard_map/pallas_call | solution.py:182
  17.3 0.0 collective-permute-done.far_ref
  17.3 2.5 %shard_map.147 = bf16[16,32,640]{2,1,0:T(8,128)(2,1)S(1)} custom-call(bf16[64,1536]{1,0:T(8,128)(2,1)S(1)} %bitcast.9, bf16[64,1536]{1,0:T(8,128)(2,1)S(1)} %collective-permute-done.far_ref, f32[3,1024]{1,0:T(4,128)S(1)} %get-tuple-element.22.xyz_ref, bf16[2,512,512]{2,1,0:T(8,128)(2,1)S(1)} %get-tuple-element.24.weights_ref, ...), custom_call_target="tpu_custom_call" | custom-call | flops 2147483648 | bytes 5242880 | tf_op jit(solution)/shard_map/pallas_call | solution.py:191
  19.8 16.2 %all_to_all.15 = bf16[16,32,640]{2,1,0:T(8,128)(2,1)S(1)} all-to-all(bf16[16,32,640]{2,1,0:T(8,128)(2,1)S(1)} %shard_map.147), channel_id=1, replica_groups=mesh['xh'=2,'z'=8,'xl'=2,'y'=4,'c'=2] {'xh','xl','y'}, dimensions={0} | all-to-all | bytes 1310720 | tf_op jit(solution)/shard_map/all_to_all | solution.py:201
  36.0 0.1 reduce_sum.12
  36.1 1.7 %collective-permute-start.1 = (bf16[32,640]{1,0:T(8,128)(2,1)S(1)}, bf16[32,640]{1,0:T(8,128)(2,1)S(1)}, u32[]{:S(2)}, u32[]{:S(2)}) collective-permute-start(bf16[32,640]{1,0:T(8,128)(2,1)S(1)} %reduce_sum.12), channel_id=1, source_target_pairs={{0,16},{16,0},{32,48},{48,32},{64,80},{80,64},{96,112},{112,96},{1... | collective-permute-start | bytes 122888 | tf_op jit(solution)/shard_map/ppermute | solution.py:143
  37.8 3.0 %collective-permute-start.2 = (bf16[32,640]{1,0:T(8,128)(2,1)S(1)}, bf16[32,640]{1,0:T(8,128)(2,1)S(1)}, u32[]{:S(2)}, u32[]{:S(2)}) collective-permute-start(bf16[32,640]{1,0:T(8,128)(2,1)S(1)} %reduce_sum.12), channel_id=1, source_target_pairs={{0,32},{16,48},{32,0},{48,16},{64,96},{80,112},{96,64},{112,80},{1... | collective-permute-start | bytes 122888 | tf_op jit(solution)/shard_map/ppermute | solution.py:143
  40.8 0.0 collective-permute-start.3
  40.8 0.0 collective-permute-done.1
  40.8 1.8 %collective-permute-done.2 = bf16[32,640]{1,0:T(8,128)(2,1)S(1)} collective-permute-done((bf16[32,640]{1,0:T(8,128)(2,1)S(1)}, bf16[32,640]{1,0:T(8,128)(2,1)S(1)}, u32[]{:S(2)}, u32[]{:S(2)}) %collective-permute-start.2) | collective-permute-done | bytes 40992 | tf_op jit(solution)/shard_map/ppermute | solution.py:143
  42.6 2.8 %collective-permute-done.3 = bf16[32,640]{1,0:T(8,128)(2,1)S(1)} collective-permute-done((bf16[32,640]{1,0:T(8,128)(2,1)S(1)}, bf16[32,640]{1,0:T(8,128)(2,1)S(1)}, u32[]{:S(2)}, u32[]{:S(2)}) %collective-permute-start.3) | collective-permute-done | bytes 40992 | tf_op jit(solution)/shard_map/ppermute | solution.py:143
  45.5 1.9 %collective-permute-start.4 = (bf16[32,640]{1,0:T(8,128)(2,1)S(1)}, bf16[32,640]{1,0:T(8,128)(2,1)S(1)}, u32[]{:S(2)}, u32[]{:S(2)}) collective-permute-start(bf16[32,640]{1,0:T(8,128)(2,1)S(1)} %add_convert_fusion.1), channel_id=1, source_target_pairs={{0,96},{16,112},{32,64},{48,80},{64,32},{80,48},{96,0},{112,16},{1... | collective-permute-start | bytes 122888 | tf_op jit(solution)/shard_map/ppermute | solution.py:143
  47.4 3.5 %collective-permute-done.4 = bf16[32,640]{1,0:T(8,128)(2,1)S(1)} collective-permute-done((bf16[32,640]{1,0:T(8,128)(2,1)S(1)}, bf16[32,640]{1,0:T(8,128)(2,1)S(1)}, u32[]{:S(2)}, u32[]{:S(2)}) %collective-permute-start.4) | collective-permute-done | bytes 40992 | tf_op jit(solution)/shard_map/ppermute | solution.py:143
  51.1 12.1 %all_to_all.16.own_ref = bf16[16,32,512]{2,1,0:T(8,128)(2,1)S(1)} all-to-all(bf16[16,32,512]{2,1,0:T(8,128)(2,1)S(1)} %broadcast_in_dim.15), channel_id=1, replica_groups=mesh['xh'=2,'z'=8,'xl'=2,'y'=4,'c'=2] {'xh','xl','y'}, dimensions={0} | all-to-all | bytes 1048576 | tf_op jit(solution)/shard_map/all_to_all | solution.py:210
  63.2 5.3 %collective-permute-start.5 = (bf16[16,32,512]{2,1,0:T(8,128)(2,1)S(1)}, bf16[16,32,512]{2,1,0:T(8,128)(2,1)S(1)}, u32[]{:S(2)}, u32[]{:S(2)}) collective-permute-start(bf16[16,32,512]{2,1,0:T(8,128)(2,1)S(1)} %all_to_all.16.own_ref), channel_id=1, source_target_pairs={{0,1},{1,0},{2,3},{3,2},{4,5},{5,4},{6,7},{7,6},{8,9},{9,8},{10,11... | collective-permute-start | bytes 1572872 | tf_op jit(solution)/shard_map/ppermute | solution.py:143
  68.5 0.0 collective-permute-start.6
  68.5 0.7 dynamic-slice_convert_fusion
  69.2 0.9 %collective-permute-done.6.other_small_ref = bf16[16,128]{1,0:T(8,128)(2,1)S(1)} collective-permute-done((bf16[16,128]{1,0:T(8,128)(2,1)S(1)}, bf16[16,128]{1,0:T(8,128)(2,1)S(1)}, u32[]{:S(2)}, u32[]{:S(2)}) %collective-permute-start.6) | collective-permute-done | bytes 4128 | tf_op jit(solution)/shard_map/ppermute | solution.py:143
  70.0 0.0 collective-permute-done.5.other_ref
  70.0 1.4 %shard_map.148 = (f32[3,512]{1,0:T(4,128)}, f32[1,512]{1,0:T(1,128)}, f32[512,512]{1,0:T(8,128)}, f32[1,512]{1,0:T(1,128)}, f32[512,512]{1,0:T(8,128)}, /*index=5*/f32[1,512]{1,0:T(1,128)}) custom-call(bf16[16,32,512]{2,1,0:T(8,128)(2,1)S(1)} %all_to_all.16.own_ref, bf16[16,32,512]{2,1,0:T(8,128)(2,1)S(1)} %collective-permute-done.5.other_ref, ...), custom_call_target="tpu_custom_call" | custom-call | tf_op jit(solution)/shard_map/pallas_call | solution.py:216
  (5 shorter events, 0.1 us)
Async XLA Ops:
  2.2 11.8 %all-to-all-start = ((bf16[8,8,1536]{2,1,0:T(8,128)(2,1)}), bf16[8,8,1536]{2,1,0:T(8,128)(2,1)S(1)}, u32[]{:S(2)}, u32[]{:S(2)}) async-start(bf16[8,8,1536]{2,1,0:T(8,128)(2,1)} %shard_map.144), calls=%async_computation | async-start | bytes 393216 | tf_op jit(solution)/shard_map/all_to_all | solution.py:161
  14.1 3.2 %collective-permute-start = (bf16[64,1536]{1,0:T(8,128)(2,1)S(1)}, bf16[64,1536]{1,0:T(8,128)(2,1)S(1)}, u32[]{:S(2)}, u32[]{:S(2)}) collective-permute-start(bf16[64,1536]{1,0:T(8,128)(2,1)S(1)} %bitcast.7), channel_id=1, source_target_pairs={{0,1},{1,0},{2,3},{3,2},{4,5},{5,4},{6,7},{7,6},{8,9},{9,8},{10,11... | collective-permute-start | bytes 589832 | tf_op jit(solution)/shard_map/ppermute | solution.py:143
  36.1 4.7 %collective-permute-start.1 = (bf16[32,640]{1,0:T(8,128)(2,1)S(1)}, bf16[32,640]{1,0:T(8,128)(2,1)S(1)}, u32[]{:S(2)}, u32[]{:S(2)}) collective-permute-start(bf16[32,640]{1,0:T(8,128)(2,1)S(1)} %reduce_sum.12), channel_id=1, source_target_pairs={{0,16},{16,0},{32,48},{48,32},{64,80},{80,64},{96,112},{112,96},{1... | collective-permute-start | bytes 122888 | tf_op jit(solution)/shard_map/ppermute | solution.py:143
  37.8 4.8 %collective-permute-start.2 = (bf16[32,640]{1,0:T(8,128)(2,1)S(1)}, bf16[32,640]{1,0:T(8,128)(2,1)S(1)}, u32[]{:S(2)}, u32[]{:S(2)}) collective-permute-start(bf16[32,640]{1,0:T(8,128)(2,1)S(1)} %reduce_sum.12), channel_id=1, source_target_pairs={{0,32},{16,48},{32,0},{48,16},{64,96},{80,112},{96,64},{112,80},{1... | collective-permute-start | bytes 122888 | tf_op jit(solution)/shard_map/ppermute | solution.py:143
  40.8 4.7 %collective-permute-start.3 = (bf16[32,640]{1,0:T(8,128)(2,1)S(1)}, bf16[32,640]{1,0:T(8,128)(2,1)S(1)}, u32[]{:S(2)}, u32[]{:S(2)}) collective-permute-start(bf16[32,640]{1,0:T(8,128)(2,1)S(1)} %reduce_sum.12), channel_id=1, source_target_pairs={{0,48},{16,32},{32,16},{48,0},{64,112},{80,96},{96,80},{112,64},{1... | collective-permute-start | bytes 122888 | tf_op jit(solution)/shard_map/ppermute | solution.py:143
  45.5 5.5 %collective-permute-start.4 = (bf16[32,640]{1,0:T(8,128)(2,1)S(1)}, bf16[32,640]{1,0:T(8,128)(2,1)S(1)}, u32[]{:S(2)}, u32[]{:S(2)}) collective-permute-start(bf16[32,640]{1,0:T(8,128)(2,1)S(1)} %add_convert_fusion.1), channel_id=1, source_target_pairs={{0,96},{16,112},{32,64},{48,80},{64,32},{80,48},{96,0},{112,16},{1... | collective-permute-start | bytes 122888 | tf_op jit(solution)/shard_map/ppermute | solution.py:143
  63.2 6.9 %collective-permute-start.5 = (bf16[16,32,512]{2,1,0:T(8,128)(2,1)S(1)}, bf16[16,32,512]{2,1,0:T(8,128)(2,1)S(1)}, u32[]{:S(2)}, u32[]{:S(2)}) collective-permute-start(bf16[16,32,512]{2,1,0:T(8,128)(2,1)S(1)} %all_to_all.16.own_ref), channel_id=1, source_target_pairs={{0,1},{1,0},{2,3},{3,2},{4,5},{5,4},{6,7},{7,6},{8,9},{9,8},{10,11... | collective-permute-start | bytes 1572872 | tf_op jit(solution)/shard_map/ppermute | solution.py:143
  68.5 1.5 %collective-permute-start.6 = (bf16[16,128]{1,0:T(8,128)(2,1)S(1)}, bf16[16,128]{1,0:T(8,128)(2,1)S(1)}, u32[]{:S(2)}, u32[]{:S(2)}) collective-permute-start(bf16[16,128]{1,0:T(8,128)(2,1)S(1)} %slice.9.own_small_ref), channel_id=1, source_target_pairs={{0,1},{1,0},{2,3},{3,2},{4,5},{5,4},{6,7},{7,6},{8,9},{9,8},{10,11... | collective-permute-start | bytes 12296 | tf_op jit(solution)/shard_map/ppermute | solution.py:143

commit v3 on v2

--- a/solution.py
+++ b/solution.py
@@ -8,7 +8,7 @@
 SPLIT = (("xh", 2), ("z", 8), ("xl", 2), ("y", 4), ("c", 2))
 AXES = tuple(name for name, _ in SPLIT)
 SIZES = tuple(size for _, size in SPLIT)
-PLANE = ("xh", "xl", "y")
+PLANE = ("xl", "xh", "y")
 VMEM_BYTES = 20 * 1024 * 1024
 BF16, F32 = jnp.bfloat16, jnp.float32
 
@@ -116,7 +116,7 @@
     small += [across(grad_basis_ref[own, :].astype(F32)), jnp.zeros((2, half), F32)]
     small = fold(jnp.concatenate(small, axis=0)).astype(BF16)
     for at in range(16):
-        group, column = at % 8, at // 8
+        group, column = at // 8 * 4 + at % 4, at // 4 % 2
         mine = coef_ref[group * 8 : group * 8 + 8, column * half : column * half + half]
         out_ref[at, :16, 512:] = fold(mine).astype(BF16)
         out_ref[at, 16:, 512:] = small
@@ -200,9 +200,9 @@
 
     parts = lax.all_to_all(partial, PLANE, 0, 0, tiled=True)
     mine = jnp.sum(parts.astype(F32), axis=0).astype(BF16)
-    one, two, three = (swap(mine, ("z", bits)).astype(F32) for bits in (1, 2, 3))
-    mine = ((mine.astype(F32) + one) + (two + three)).astype(BF16)
-    mine = (mine.astype(F32) + swap(mine, ("z", 6)).astype(F32)).astype(BF16)
+    three, two, one = (swap(mine, ("z", bits)).astype(F32) for bits in (3, 2, 1))
+    mine = (((three + two) + (one + mine.astype(F32)))).astype(BF16)
+    mine = (mine.astype(F32) + swap(mine, ("z", 7)).astype(F32)).astype(BF16)
 
     small = mine[16:, 512:]
     other_small = swap(small, ("c", 1))

time: 71.8 us -> 69 us (0.961)
  waiting for transfers between devices: 11.6 us -> 8.14 us
  starting transfers between devices: 20 us -> 20.8 us
    ppermute x7, waiting for transfers between devices: 9.08 us -> 5.64 us  [swap(): lax.ppermute(value, axis, [(i, i ^ bits) for i in range(dict(SPLIT)[axis])])]
    ppermute x7, starting transfers between devices: 14 us -> 14.8 us  [swap(): lax.ppermute(value, axis, [(i, i ^ bits) for i in range(dict(SPLIT)[axis])])]
  transfers between devices with their start and end apart: 8 -> 8, of which waited for: 5 -> 5; matrix products, arithmetic and copies ran while one was open for 1% -> 1% of each run, Pallas kernels for 6% -> 7%
where the time goes in v3:
time: 69 us; the launch traced here: 68.7 us
  blocking collectives  28.1 us (41%)
  starting transfers between devices  20.8 us (30%)
  Pallas kernels  10.1 us (15%)
  waiting for transfers between devices  8.14 us (12%)
  other arithmetic  0.8 us (1%)
    all_to_all x1, blocking collectives, shards(): parts = lax.all_to_all(partial, PLANE, 0, 0, tiled=True)  16.4 us
    ppermute x7, starting transfers between devices, swap(): lax.ppermute(value, axis, [(i, i ^ bits) for i in range(dict(SPLIT)[axis])])  14.8 us
    all_to_all x1, blocking collectives, shards(): gathered = lax.all_to_all(gathered, PLANE, 0, 0, tiled=True)  11.8 us
    all_to_all x1, starting transfers between devices, shards(): lax.all_to_all(send, ('xl', 'y'), 0, 0, tiled=True)  5.95 us
    ppermute x7, waiting for transfers between devices, swap(): lax.ppermute(value, axis, [(i, i ^ bits) for i in range(dict(SPLIT)[axis])])  5.64 us
    pallas_call x1, Pallas kernels, shards(): pl.pallas_call(forward_kernel, out_shape=(pltpu.VMEM((2, 512, points), BF...  3.37 us
    all_to_all x1, waiting for transfers between devices, shards(): lax.all_to_all(send, ('xl', 'y'), 0, 0, tiled=True)  2.5 us
    pallas_call x1, Pallas kernels, shards(): pl.pallas_call(backward_kernel, out_shape=jax.ShapeDtypeStruct((16, 32, 6...  2.49 us
  transfers between devices with their start and end apart: 8, of which 5 were waited for; matrix products, arithmetic and copies ran while one was open for 1% of the time, Pallas kernels for 7%

profile of v3, /device:TPU:1, one launch (start us, length us, event | category | flops | bytes accessed | tf_op | source)
XLA Modules:
  0.0 68.7 jit_solution(11670952839042681723)
XLA Ops:
  0.6 1.6 %shard_map.144 = bf16[8,8,1536]{2,1,0:T(8,128)(2,1)} custom-call(bf16[8,8192]{1,0:T(8,128)(2,1)} %grad_out_ref.1, bf16[8,512]{1,0:T(8,128)(2,1)} %coef_ref.1), custom_call_target="tpu_custom_call" | custom-call | tf_op jit(solution)/shard_map/pallas_call | solution.py:155
  2.2 5.9 %all-to-all-start = ((bf16[8,8,1536]{2,1,0:T(8,128)(2,1)}), bf16[8,8,1536]{2,1,0:T(8,128)(2,1)S(1)}, u32[]{:S(2)}, u32[]{:S(2)}) async-start(bf16[8,8,1536]{2,1,0:T(8,128)(2,1)} %shard_map.144), calls=%async_computation | async-start | bytes 393216 | tf_op jit(solution)/shard_map/all_to_all | solution.py:161
  8.2 3.4 %shard_map.145 = (bf16[2,512,1024]{2,1,0:T(8,128)(2,1)S(1)}, bf16[512,1024]{1,0:T(8,128)(2,1)S(1)}, f32[3,1024]{1,0:T(4,128)S(1)}) custom-call(f32[3,8192]{1,0:T(4,128)} %coords_ref.1, f32[3,512]{1,0:T(4,128)} %w_first_ref.1, f32[1,512]{1,0:T(1,128)} %bitcast.10, bf16[512,512]{1,0:T(8,128)(2,1)} %w_second_ref.3, f32[1,512]{1,0:T(1,128)} %bitcast.11, ...), custom_call_target="tpu_custom_call" | custom-call | flops 1073741824 | bytes 5242880 | tf_op jit(solution)/shard_map/pallas_call | solution.py:162
  11.6 2.5 %all-to-all-done = bf16[8,8,1536]{2,1,0:T(8,128)(2,1)S(1)} async-done(((bf16[8,8,1536]{2,1,0:T(8,128)(2,1)}), bf16[8,8,1536]{2,1,0:T(8,128)(2,1)S(1)}, u32[]{:S(2)}, u32[]{:S(2)}) %all-to-all-start) | async-done | bytes 196640 | tf_op jit(solution)/shard_map/all_to_all | solution.py:161
  14.1 2.0 %collective-permute-start = (bf16[64,1536]{1,0:T(8,128)(2,1)S(1)}, bf16[64,1536]{1,0:T(8,128)(2,1)S(1)}, u32[]{:S(2)}, u32[]{:S(2)}) collective-permute-start(bf16[64,1536]{1,0:T(8,128)(2,1)S(1)} %bitcast.7), channel_id=1, source_target_pairs={{0,1},{1,0},{2,3},{3,2},{4,5},{5,4},{6,7},{7,6},{8,9},{9,8},{10,11... | collective-permute-start | bytes 589832 | tf_op jit(solution)/shard_map/ppermute | solution.py:143
  16.1 1.2 %shard_map.146 = (f32[64,512]{1,0:T(8,128)S(1)}, bf16[2,512,512]{2,1,0:T(8,128)(2,1)S(1)}) custom-call(bf16[64,1536]{1,0:T(8,128)(2,1)S(1)} %bitcast.8, bf16[512,1024]{1,0:T(8,128)(2,1)S(1)} %get-tuple-element.23.basis_ref, bf16[512,512]{1,0:T(8,128)(2,1)} %w_second_ref.3, bf16[512,512]{1,0:T(8,128)(2,1)} %w_third_ref.3), custom_call_target="tpu_custom_call" | custom-call | flops 268435456 | bytes 2097152 | tf_op jit(solution)/shard_map/pallas_call | solution.py:182
  17.3 0.0 collective-permute-done.far_ref
  17.3 2.5 %shard_map.147 = bf16[16,32,640]{2,1,0:T(8,128)(2,1)S(1)} custom-call(bf16[64,1536]{1,0:T(8,128)(2,1)S(1)} %bitcast.9, bf16[64,1536]{1,0:T(8,128)(2,1)S(1)} %collective-permute-done.far_ref, f32[3,1024]{1,0:T(4,128)S(1)} %get-tuple-element.22.xyz_ref, bf16[2,512,512]{2,1,0:T(8,128)(2,1)S(1)} %get-tuple-element.24.weights_ref, ...), custom_call_target="tpu_custom_call" | custom-call | flops 2147483648 | bytes 5242880 | tf_op jit(solution)/shard_map/pallas_call | solution.py:191
  19.8 16.4 %all_to_all.15 = bf16[16,32,640]{2,1,0:T(8,128)(2,1)S(1)} all-to-all(bf16[16,32,640]{2,1,0:T(8,128)(2,1)S(1)} %shard_map.147), channel_id=1, replica_groups=mesh['xh'=2,'z'=8,'xl'=2,'y'=4,'c'=2] {'xl','xh','y'}, dimensions={0} | all-to-all | bytes 1310720 | tf_op jit(solution)/shard_map/all_to_all | solution.py:201
  36.2 0.1 reduce_sum.12
  36.3 4.4 %collective-permute-start.1 = (bf16[32,640]{1,0:T(8,128)(2,1)S(1)}, bf16[32,640]{1,0:T(8,128)(2,1)S(1)}, u32[]{:S(2)}, u32[]{:S(2)}) collective-permute-start(bf16[32,640]{1,0:T(8,128)(2,1)S(1)} %reduce_sum.12), channel_id=1, source_target_pairs={{0,48},{16,32},{32,16},{48,0},{64,112},{80,96},{96,80},{112,64},{1... | collective-permute-start | bytes 122888 | tf_op jit(solution)/shard_map/ppermute | solution.py:143
  40.7 0.0 collective-permute-start.2
  40.7 0.4 collective-permute-start.3
  41.1 1.0 %collective-permute-done.1 = bf16[32,640]{1,0:T(8,128)(2,1)S(1)} collective-permute-done((bf16[32,640]{1,0:T(8,128)(2,1)S(1)}, bf16[32,640]{1,0:T(8,128)(2,1)S(1)}, u32[]{:S(2)}, u32[]{:S(2)}) %collective-permute-start.1) | collective-permute-done | bytes 40992 | tf_op jit(solution)/shard_map/ppermute | solution.py:143
  42.1 2.4 %collective-permute-done.2 = bf16[32,640]{1,0:T(8,128)(2,1)S(1)} collective-permute-done((bf16[32,640]{1,0:T(8,128)(2,1)S(1)}, bf16[32,640]{1,0:T(8,128)(2,1)S(1)}, u32[]{:S(2)}, u32[]{:S(2)}) %collective-permute-start.2) | collective-permute-done | bytes 40992 | tf_op jit(solution)/shard_map/ppermute | solution.py:143
  44.5 0.0 collective-permute-done.3
  44.5 3.5 %collective-permute-start.4 = (bf16[32,640]{1,0:T(8,128)(2,1)S(1)}, bf16[32,640]{1,0:T(8,128)(2,1)S(1)}, u32[]{:S(2)}, u32[]{:S(2)}) collective-permute-start(bf16[32,640]{1,0:T(8,128)(2,1)S(1)} %add_convert_fusion.1), channel_id=1, source_target_pairs={{0,112},{16,96},{32,80},{48,64},{64,48},{80,32},{96,16},{112,0},{1... | collective-permute-start | bytes 122888 | tf_op jit(solution)/shard_map/ppermute | solution.py:143
  48.0 1.4 %collective-permute-done.4 = bf16[32,640]{1,0:T(8,128)(2,1)S(1)} collective-permute-done((bf16[32,640]{1,0:T(8,128)(2,1)S(1)}, bf16[32,640]{1,0:T(8,128)(2,1)S(1)}, u32[]{:S(2)}, u32[]{:S(2)}) %collective-permute-start.4) | collective-permute-done | bytes 40992 | tf_op jit(solution)/shard_map/ppermute | solution.py:143
  49.5 11.8 %all_to_all.16.own_ref = bf16[16,32,512]{2,1,0:T(8,128)(2,1)S(1)} all-to-all(bf16[16,32,512]{2,1,0:T(8,128)(2,1)S(1)} %broadcast_in_dim.15), channel_id=1, replica_groups=mesh['xh'=2,'z'=8,'xl'=2,'y'=4,'c'=2] {'xl','xh','y'}, dimensions={0} | all-to-all | bytes 1048576 | tf_op jit(solution)/shard_map/all_to_all | solution.py:210
  61.3 4.5 %collective-permute-start.5 = (bf16[16,32,512]{2,1,0:T(8,128)(2,1)S(1)}, bf16[16,32,512]{2,1,0:T(8,128)(2,1)S(1)}, u32[]{:S(2)}, u32[]{:S(2)}) collective-permute-start(bf16[16,32,512]{2,1,0:T(8,128)(2,1)S(1)} %all_to_all.16.own_ref), channel_id=1, source_target_pairs={{0,1},{1,0},{2,3},{3,2},{4,5},{5,4},{6,7},{7,6},{8,9},{9,8},{10,11... | collective-permute-start | bytes 1572872 | tf_op jit(solution)/shard_map/ppermute | solution.py:143
  65.8 0.0 collective-permute-start.6
  65.8 0.7 dynamic-slice_convert_fusion
  66.4 0.9 %collective-permute-done.6.other_small_ref = bf16[16,128]{1,0:T(8,128)(2,1)S(1)} collective-permute-done((bf16[16,128]{1,0:T(8,128)(2,1)S(1)}, bf16[16,128]{1,0:T(8,128)(2,1)S(1)}, u32[]{:S(2)}, u32[]{:S(2)}) %collective-permute-start.6) | collective-permute-done | bytes 4128 | tf_op jit(solution)/shard_map/ppermute | solution.py:143
  67.3 0.0 collective-permute-done.5.other_ref
  67.3 1.4 %shard_map.148 = (f32[3,512]{1,0:T(4,128)}, f32[1,512]{1,0:T(1,128)}, f32[512,512]{1,0:T(8,128)}, f32[1,512]{1,0:T(1,128)}, f32[512,512]{1,0:T(8,128)}, /*index=5*/f32[1,512]{1,0:T(1,128)}) custom-call(bf16[16,32,512]{2,1,0:T(8,128)(2,1)S(1)} %all_to_all.16.own_ref, bf16[16,32,512]{2,1,0:T(8,128)(2,1)S(1)} %collective-permute-done.5.other_ref, ...), custom_call_target="tpu_custom_call" | custom-call | tf_op jit(solution)/shard_map/pallas_call | solution.py:216
  (5 shorter events, 0.1 us)
Async XLA Ops:
  2.2 11.8 %all-to-all-start = ((bf16[8,8,1536]{2,1,0:T(8,128)(2,1)}), bf16[8,8,1536]{2,1,0:T(8,128)(2,1)S(1)}, u32[]{:S(2)}, u32[]{:S(2)}) async-start(bf16[8,8,1536]{2,1,0:T(8,128)(2,1)} %shard_map.144), calls=%async_computation | async-start | bytes 393216 | tf_op jit(solution)/shard_map/all_to_all | solution.py:161
  14.1 3.2 %collective-permute-start = (bf16[64,1536]{1,0:T(8,128)(2,1)S(1)}, bf16[64,1536]{1,0:T(8,128)(2,1)S(1)}, u32[]{:S(2)}, u32[]{:S(2)}) collective-permute-start(bf16[64,1536]{1,0:T(8,128)(2,1)S(1)} %bitcast.7), channel_id=1, source_target_pairs={{0,1},{1,0},{2,3},{3,2},{4,5},{5,4},{6,7},{7,6},{8,9},{9,8},{10,11... | collective-permute-start | bytes 589832 | tf_op jit(solution)/shard_map/ppermute | solution.py:143
  36.3 5.8 %collective-permute-start.1 = (bf16[32,640]{1,0:T(8,128)(2,1)S(1)}, bf16[32,640]{1,0:T(8,128)(2,1)S(1)}, u32[]{:S(2)}, u32[]{:S(2)}) collective-permute-start(bf16[32,640]{1,0:T(8,128)(2,1)S(1)} %reduce_sum.12), channel_id=1, source_target_pairs={{0,48},{16,32},{32,16},{48,0},{64,112},{80,96},{96,80},{112,64},{1... | collective-permute-start | bytes 122888 | tf_op jit(solution)/shard_map/ppermute | solution.py:143
  40.7 3.8 %collective-permute-start.2 = (bf16[32,640]{1,0:T(8,128)(2,1)S(1)}, bf16[32,640]{1,0:T(8,128)(2,1)S(1)}, u32[]{:S(2)}, u32[]{:S(2)}) collective-permute-start(bf16[32,640]{1,0:T(8,128)(2,1)S(1)} %reduce_sum.12), channel_id=1, source_target_pairs={{0,32},{16,48},{32,0},{48,16},{64,96},{80,112},{96,64},{112,80},{1... | collective-permute-start | bytes 122888 | tf_op jit(solution)/shard_map/ppermute | solution.py:143
  40.7 3.8 %collective-permute-start.3 = (bf16[32,640]{1,0:T(8,128)(2,1)S(1)}, bf16[32,640]{1,0:T(8,128)(2,1)S(1)}, u32[]{:S(2)}, u32[]{:S(2)}) collective-permute-start(bf16[32,640]{1,0:T(8,128)(2,1)S(1)} %reduce_sum.12), channel_id=1, source_target_pairs={{0,16},{16,0},{32,48},{48,32},{64,80},{80,64},{96,112},{112,96},{1... | collective-permute-start | bytes 122888 | tf_op jit(solution)/shard_map/ppermute | solution.py:143
  44.5 4.9 %collective-permute-start.4 = (bf16[32,640]{1,0:T(8,128)(2,1)S(1)}, bf16[32,640]{1,0:T(8,128)(2,1)S(1)}, u32[]{:S(2)}, u32[]{:S(2)}) collective-permute-start(bf16[32,640]{1,0:T(8,128)(2,1)S(1)} %add_convert_fusion.1), channel_id=1, source_target_pairs={{0,112},{16,96},{32,80},{48,64},{64,48},{80,32},{96,16},{112,0},{1... | collective-permute-start | bytes 122888 | tf_op jit(solution)/shard_map/ppermute | solution.py:143
  61.3 6.0 %collective-permute-start.5 = (bf16[16,32,512]{2,1,0:T(8,128)(2,1)S(1)}, bf16[16,32,512]{2,1,0:T(8,128)(2,1)S(1)}, u32[]{:S(2)}, u32[]{:S(2)}) collective-permute-start(bf16[16,32,512]{2,1,0:T(8,128)(2,1)S(1)} %all_to_all.16.own_ref), channel_id=1, source_target_pairs={{0,1},{1,0},{2,3},{3,2},{4,5},{5,4},{6,7},{7,6},{8,9},{9,8},{10,11... | collective-permute-start | bytes 1572872 | tf_op jit(solution)/shard_map/ppermute | solution.py:143
  65.8 1.5 %collective-permute-start.6 = (bf16[16,128]{1,0:T(8,128)(2,1)S(1)}, bf16[16,128]{1,0:T(8,128)(2,1)S(1)}, u32[]{:S(2)}, u32[]{:S(2)}) collective-permute-start(bf16[16,128]{1,0:T(8,128)(2,1)S(1)} %slice.9.own_small_ref), channel_id=1, source_target_pairs={{0,1},{1,0},{2,3},{3,2},{4,5},{5,4},{6,7},{7,6},{8,9},{9,8},{10,11... | collective-permute-start | bytes 12296 | tf_op jit(solution)/shard_map/ppermute | solution.py:143

commit v4 on v3

--- a/solution.py
+++ b/solution.py
@@ -92,7 +92,8 @@
 
 
 def backward_kernel(
-    near_ref, far_ref, xyz_ref, weights_ref, coef_ref, acts_ref, out_ref, grad_basis_ref, pre_two_ref
+    near_ref, far_ref, xyz_ref, weights_ref, coef_ref, acts_ref, out_ref, grad_basis_ref, pre_two_ref,
+    pre_one_ref,
 ):
     one_ref, two_ref = acts_ref.at[0], acts_ref.at[1]
     w_second_ref, w_third_ref = weights_ref.at[0], weights_ref.at[1]
@@ -103,14 +104,14 @@
     grad_basis = tn(near_ref[:, points:], near_ref[:, :points])
     grad_basis = grad_basis + tn(far_ref[:, points:], far_ref[:, :points])
     grad_basis_ref[...] = grad_basis.astype(BF16)
-    out_ref[:, :16, :512] = nt(two_ref[own, :], grad_basis_ref[...]).astype(BF16).reshape(16, 16, 512)
     two = two_ref[...].astype(F32)
     pre_two_ref[...] = (nn(w_third_ref[...], grad_basis_ref[...]) * (1.0 - two * two)).astype(BF16)
+    one = one_ref[own, :].astype(F32)
+    pre_one_ref[...] = nn(w_second_ref[own, :], pre_two_ref[...]) * (1.0 - one * one)
+    out_ref[:, :16, :512] = nt(two_ref[own, :], grad_basis_ref[...]).astype(BF16).reshape(16, 16, 512)
     out_ref[:, 16:, :512] = nt(one_ref[own, :], pre_two_ref[...]).astype(BF16).reshape(16, 16, 512)
-    one = one_ref[own, :].astype(F32)
-    pre_one = nn(w_second_ref[own, :], pre_two_ref[...]) * (1.0 - one * one)
-
-    xyz = xyz_ref[...]
+
+    xyz, pre_one = xyz_ref[...], pre_one_ref[...]
     small = [across(pre_one * xyz[axis : axis + 1]) for axis in range(3)]
     small += [across(pre_one), across(pre_two_ref[own, :].astype(F32))]
     small += [across(grad_basis_ref[own, :].astype(F32)), jnp.zeros((2, half), F32)]
@@ -122,20 +123,49 @@
         out_ref[at, 16:, 512:] = small
 
 
-def finish_kernel(
-    own_ref, other_ref, own_small_ref, other_small_ref, w_first_ref, b_first_ref, w_second_ref,
-    b_second_ref, w_third_ref, b_third_ref,
+def widen(at, blocks_ref, wide_ref, w_second_ref, w_third_ref, sems):
+    half = wide_ref.shape[1]
+    where = pl.ds(pl.multiple_of(at * half, half), half)
+    copies = []
+    for which, out_ref in enumerate((w_third_ref, w_second_ref)):
+        value = blocks_ref[:, 16 * which : 16 * which + 16, :]
+        wide_ref[which] = value.reshape(half, 512).astype(F32)
+        copies.append(pltpu.make_async_copy(wide_ref.at[which], out_ref.at[where, :], sems.at[which]))
+        copies[-1].start()
+    return copies
+
+
+def own_kernel(own_ref, sums_ref, w_second_ref, w_third_ref, coef_ref, wide_ref, mine_ref, sems):
+    copies = widen(lax.axis_index("c"), own_ref, wide_ref, w_second_ref, w_third_ref, sems)
+    row = lax.broadcasted_iota(jnp.int32, (256, 32), 0)
+    column = lax.broadcasted_iota(jnp.int32, (256, 32), 1)
+    chosen = (row == column + lax.axis_index("z") * 32).astype(F32).astype(BF16)
+    mine_ref[...] = nn(unfold(sums_ref[:16, 512:].astype(F32)).astype(BF16), chosen)
+    copies.append(pltpu.make_async_copy(mine_ref, coef_ref, sems.at[2]))
+    copies[-1].start()
+    for copy in copies:
+        copy.wait()
+
+
+def other_kernel(
+    other_ref, own_small_ref, other_small_ref, w_second_in_ref, w_third_in_ref, w_second_ref, w_third_ref,
+    w_first_ref, b_first_ref, b_second_ref, b_third_ref, wide_ref, small_ref, first_ref, sems,
 ):
-    core, half = lax.axis_index("c"), 256
-    for at, ref, small_ref in ((core, own_ref, own_small_ref), (1 - core, other_ref, other_small_ref)):
+    core, half = lax.axis_index("c"), wide_ref.shape[1]
+    for at, ref in ((core, own_small_ref), (1 - core, other_small_ref)):
         where = pl.ds(pl.multiple_of(at * half, half), half)
-        w_third_ref[where, :] = ref[:, :16, :].reshape(half, 512).astype(F32)
-        w_second_ref[where, :] = ref[:, 16:, :].reshape(half, 512).astype(F32)
-        small = unfold(small_ref[...].astype(F32))
-        w_first_ref[:, where] = small[0:3]
-        b_first_ref[:, where] = small[3:4]
-        b_second_ref[:, where] = small[4:5]
-        b_third_ref[:, where] = small[5:6]
+        small = unfold(ref[...].astype(F32))
+        first_ref[:, where] = small[0:3]
+        for which in range(3):
+            small_ref[which, :, where] = small[3 + which : 4 + which]
+    copies = [pltpu.make_async_copy(first_ref, w_first_ref, sems.at[2])]
+    for which, out_ref in enumerate((b_first_ref, b_second_ref, b_third_ref)):
+        copies.append(pltpu.make_async_copy(small_ref.at[which], out_ref, sems.at[3 + which]))
+    for copy in copies:
+        copy.start()
+    copies += widen(1 - core, other_ref, wide_ref, w_second_ref, w_third_ref, sems)
+    for copy in copies:
+        copy.wait()
 
 
 def swap(value, flip):
@@ -193,7 +223,7 @@
         out_shape=jax.ShapeDtypeStruct((16, 32, 640), BF16),
         in_specs=[vmem] * 6,
         out_specs=vmem,
-        scratch_shapes=[pltpu.VMEM((512, points), BF16)] * 2,
+        scratch_shapes=[pltpu.VMEM((512, points), BF16)] * 2 + [pltpu.VMEM((256, points), F32)],
         compiler_params=pltpu.CompilerParams(vmem_limit_bytes=VMEM_BYTES),
         cost_estimate=pl.CostEstimate(flops=2**31, bytes_accessed=5 * 2**20, transcendentals=0),
     )(near, far, xyz, weights, coef_part, acts)
@@ -201,7 +231,7 @@
     parts = lax.all_to_all(partial, PLANE, 0, 0, tiled=True)
     mine = jnp.sum(parts.astype(F32), axis=0).astype(BF16)
     three, two, one = (swap(mine, ("z", bits)).astype(F32) for bits in (3, 2, 1))
-    mine = (((three + two) + (one + mine.astype(F32)))).astype(BF16)
+    mine = ((one + mine.astype(F32)) + (two + three)).astype(BF16)
     mine = (mine.astype(F32) + swap(mine, ("z", 7)).astype(F32)).astype(BF16)
 
     small = mine[16:, 512:]
@@ -209,17 +239,33 @@
     gathered = jnp.broadcast_to(mine[:, :512], (16, 32, 512))
     gathered = lax.all_to_all(gathered, PLANE, 0, 0, tiled=True)
     other = swap(gathered, ("c", 1))
-    row = jax.ShapeDtypeStruct((1, 512), F32)
-    square = jax.ShapeDtypeStruct((512, 512), F32)
-    z = lax.axis_index("z")
-    grad_coef = lax.dynamic_slice(mine, (z // 4 * 8, 512 + z % 4 * 32), (8, 32)).astype(F32)
-    w_one, b_one, w_two, b_two, w_three, b_three = pl.pallas_call(
-        finish_kernel,
-        out_shape=(jax.ShapeDtypeStruct((3, 512), F32), row, square, row, square, row),
-        in_specs=[vmem] * 4,
-        out_specs=(vmem,) * 6,
-        compiler_params=pltpu.CompilerParams(vmem_limit_bytes=VMEM_BYTES),
-    )(gathered, other, small, other_small)
+    row, square = pltpu.HBM((1, 512), F32), pltpu.HBM((512, 512), F32)
+    wide = pltpu.VMEM((2, 256, 512), F32)
+    cost = pl.CostEstimate(flops=2**20, bytes_accessed=2**21, transcendentals=0)
+    w_two, w_three, grad_coef = pl.pallas_call(
+        own_kernel,
+        out_shape=(square, square, pltpu.HBM((8, 32), F32)),
+        in_specs=[vmem, vmem],
+        out_specs=(hbm,) * 3,
+        scratch_shapes=[wide, pltpu.VMEM((8, 32), F32), pltpu.SemaphoreType.DMA((3,))],
+        compiler_params=pltpu.CompilerParams(vmem_limit_bytes=VMEM_BYTES),
+        cost_estimate=cost,
+    )(gathered, mine)
+    w_two, w_three, w_one, b_one, b_two, b_three = pl.pallas_call(
+        other_kernel,
+        out_shape=(square, square, pltpu.HBM((3, 512), F32), row, row, row),
+        in_specs=[vmem, vmem, vmem, hbm, hbm],
+        out_specs=(hbm,) * 6,
+        input_output_aliases={3: 0, 4: 1},
+        scratch_shapes=[
+            wide,
+            pltpu.VMEM((3, 1, 512), F32),
+            pltpu.VMEM((3, 512), F32),
+            pltpu.SemaphoreType.DMA((6,)),
+        ],
+        compiler_params=pltpu.CompilerParams(vmem_limit_bytes=VMEM_BYTES),
+        cost_estimate=cost,
+    )(other, small, other_small, w_two, w_three)
     return (grad_coef, w_one, b_one[0], w_two, b_two[0], w_three, b_three[0])
 
 

time: 69 us -> 68.5 us (level)
    pallas_call x1 -> x2, Pallas kernels: 1.43 us -> 2.1 us  [the longest x1 1.06 us: shards(): pl.pallas_call(other_kernel, out_shape=(square, square, pltpu.HBM((3, 512...]
  transfers between devices with their start and end apart: 8 -> 8, of which waited for: 5 -> 5; matrix products, arithmetic and copies ran while one was open for 1% -> 0% of each run, Pallas kernels for 7% -> 8%
where the time goes in v4:
time: 68.5 us; the launch traced here: 68.2 us
  blocking collectives  28.1 us (41%)
  starting transfers between devices  20.8 us (30%)
  Pallas kernels  10.6 us (15%)
  waiting for transfers between devices  7.76 us (11%)
  between operations  0.71 us (1%)
    all_to_all x1, blocking collectives, shards(): parts = lax.all_to_all(partial, PLANE, 0, 0, tiled=True)  16.4 us
    ppermute x7, starting transfers between devices, swap(): lax.ppermute(value, axis, [(i, i ^ bits) for i in range(dict(SPLIT)[axis])])  14.9 us
    all_to_all x1, blocking collectives, shards(): gathered = lax.all_to_all(gathered, PLANE, 0, 0, tiled=True)  11.8 us
    all_to_all x1, starting transfers between devices, shards(): lax.all_to_all(send, ('xl', 'y'), 0, 0, tiled=True)  5.95 us
    ppermute x7, waiting for transfers between devices, swap(): lax.ppermute(value, axis, [(i, i ^ bits) for i in range(dict(SPLIT)[axis])])  5.26 us
    pallas_call x1, Pallas kernels, shards(): pl.pallas_call(forward_kernel, out_shape=(pltpu.VMEM((2, 512, points), BF...  3.37 us
    all_to_all x1, waiting for transfers between devices, shards(): lax.all_to_all(send, ('xl', 'y'), 0, 0, tiled=True)  2.5 us
    pallas_call x1, Pallas kernels, shards(): pl.pallas_call(backward_kernel, out_shape=jax.ShapeDtypeStruct((16, 32, 6...  2.35 us
  transfers between devices with their start and end apart: 8, of which 5 were waited for; matrix products, arithmetic and copies ran while one was open for 0% of the time, Pallas kernels for 8%

profile of v4, /device:TPU:1, one launch (start us, length us, event | category | flops | bytes accessed | tf_op | source)
XLA Modules:
  0.0 68.2 jit_solution(15899742227236319283)
XLA Ops:
  0.6 1.6 %shard_map.144 = bf16[8,8,1536]{2,1,0:T(8,128)(2,1)} custom-call(bf16[8,8192]{1,0:T(8,128)(2,1)} %grad_out_ref.1, bf16[8,512]{1,0:T(8,128)(2,1)} %coef_ref.1), custom_call_target="tpu_custom_call" | custom-call | tf_op jit(solution)/shard_map/pallas_call | solution.py:185
  2.2 5.9 %all-to-all-start = ((bf16[8,8,1536]{2,1,0:T(8,128)(2,1)}), bf16[8,8,1536]{2,1,0:T(8,128)(2,1)S(1)}, u32[]{:S(2)}, u32[]{:S(2)}) async-start(bf16[8,8,1536]{2,1,0:T(8,128)(2,1)} %shard_map.144), calls=%async_computation | async-start | bytes 393216 | tf_op jit(solution)/shard_map/all_to_all | solution.py:191
  8.2 3.4 %shard_map.145 = (bf16[2,512,1024]{2,1,0:T(8,128)(2,1)S(1)}, bf16[512,1024]{1,0:T(8,128)(2,1)S(1)}, f32[3,1024]{1,0:T(4,128)S(1)}) custom-call(f32[3,8192]{1,0:T(4,128)} %coords_ref.1, f32[3,512]{1,0:T(4,128)} %w_first_ref.1, f32[1,512]{1,0:T(1,128)} %bitcast.10, bf16[512,512]{1,0:T(8,128)(2,1)} %w_second_ref.3, f32[1,512]{1,0:T(1,128)} %bitcast.11, ...), custom_call_target="tpu_custom_call" | custom-call | flops 1073741824 | bytes 5242880 | tf_op jit(solution)/shard_map/pallas_call | solution.py:192
  11.6 2.5 %all-to-all-done = bf16[8,8,1536]{2,1,0:T(8,128)(2,1)S(1)} async-done(((bf16[8,8,1536]{2,1,0:T(8,128)(2,1)}), bf16[8,8,1536]{2,1,0:T(8,128)(2,1)S(1)}, u32[]{:S(2)}, u32[]{:S(2)}) %all-to-all-start) | async-done | bytes 196640 | tf_op jit(solution)/shard_map/all_to_all | solution.py:191
  14.1 2.0 %collective-permute-start = (bf16[64,1536]{1,0:T(8,128)(2,1)S(1)}, bf16[64,1536]{1,0:T(8,128)(2,1)S(1)}, u32[]{:S(2)}, u32[]{:S(2)}) collective-permute-start(bf16[64,1536]{1,0:T(8,128)(2,1)S(1)} %bitcast.7), channel_id=1, source_target_pairs={{0,1},{1,0},{2,3},{3,2},{4,5},{5,4},{6,7},{7,6},{8,9},{9,8},{10,11... | collective-permute-start | bytes 589832 | tf_op jit(solution)/shard_map/ppermute | solution.py:173
  16.1 1.2 %shard_map.146 = (f32[64,512]{1,0:T(8,128)S(1)}, bf16[2,512,512]{2,1,0:T(8,128)(2,1)S(1)}) custom-call(bf16[64,1536]{1,0:T(8,128)(2,1)S(1)} %bitcast.8, bf16[512,1024]{1,0:T(8,128)(2,1)S(1)} %get-tuple-element.26.basis_ref, bf16[512,512]{1,0:T(8,128)(2,1)} %w_second_ref.3, bf16[512,512]{1,0:T(8,128)(2,1)} %w_third_ref.3), custom_call_target="tpu_custom_call" | custom-call | flops 268435456 | bytes 2097152 | tf_op jit(solution)/shard_map/pallas_call | solution.py:212
  17.3 0.0 collective-permute-done.far_ref
  17.3 2.4 %shard_map.147 = bf16[16,32,640]{2,1,0:T(8,128)(2,1)S(1)} custom-call(bf16[64,1536]{1,0:T(8,128)(2,1)S(1)} %bitcast.9, bf16[64,1536]{1,0:T(8,128)(2,1)S(1)} %collective-permute-done.far_ref, f32[3,1024]{1,0:T(4,128)S(1)} %get-tuple-element.25.xyz_ref, bf16[2,512,512]{2,1,0:T(8,128)(2,1)S(1)} %get-tuple-element.27.weights_ref, ...), custom_call_target="tpu_custom_call" | custom-call | flops 2147483648 | bytes 5242880 | tf_op jit(solution)/shard_map/pallas_call | solution.py:221
  19.7 16.4 %all_to_all.15 = bf16[16,32,640]{2,1,0:T(8,128)(2,1)S(1)} all-to-all(bf16[16,32,640]{2,1,0:T(8,128)(2,1)S(1)} %shard_map.147), channel_id=1, replica_groups=mesh['xh'=2,'z'=8,'xl'=2,'y'=4,'c'=2] {'xl','xh','y'}, dimensions={0} | all-to-all | bytes 1310720 | tf_op jit(solution)/shard_map/all_to_all | solution.py:231
  36.0 0.1 reduce_sum.12
  36.1 4.4 %collective-permute-start.3 = (bf16[32,640]{1,0:T(8,128)(2,1)S(1)}, bf16[32,640]{1,0:T(8,128)(2,1)S(1)}, u32[]{:S(2)}, u32[]{:S(2)}) collective-permute-start(bf16[32,640]{1,0:T(8,128)(2,1)S(1)} %reduce_sum.12), channel_id=1, source_target_pairs={{0,48},{16,32},{32,16},{48,0},{64,112},{80,96},{96,80},{112,64},{1... | collective-permute-start | bytes 122888 | tf_op jit(solution)/shard_map/ppermute | solution.py:173
  40.6 0.0 collective-permute-start.2
  40.6 0.4 collective-permute-start.1
  40.9 1.0 %collective-permute-done.3 = bf16[32,640]{1,0:T(8,128)(2,1)S(1)} collective-permute-done((bf16[32,640]{1,0:T(8,128)(2,1)S(1)}, bf16[32,640]{1,0:T(8,128)(2,1)S(1)}, u32[]{:S(2)}, u32[]{:S(2)}) %collective-permute-start.3) | collective-permute-done | bytes 40992 | tf_op jit(solution)/shard_map/ppermute | solution.py:173
  42.0 2.4 %collective-permute-done.2 = bf16[32,640]{1,0:T(8,128)(2,1)S(1)} collective-permute-done((bf16[32,640]{1,0:T(8,128)(2,1)S(1)}, bf16[32,640]{1,0:T(8,128)(2,1)S(1)}, u32[]{:S(2)}, u32[]{:S(2)}) %collective-permute-start.2) | collective-permute-done | bytes 40992 | tf_op jit(solution)/shard_map/ppermute | solution.py:173
  44.3 0.0 collective-permute-done.1
  44.3 3.5 %collective-permute-start.4 = (bf16[32,640]{1,0:T(8,128)(2,1)S(1)}, bf16[32,640]{1,0:T(8,128)(2,1)S(1)}, u32[]{:S(2)}, u32[]{:S(2)}) collective-permute-start(bf16[32,640]{1,0:T(8,128)(2,1)S(1)} %add_convert_fusion.1), channel_id=1, source_target_pairs={{0,112},{16,96},{32,80},{48,64},{64,48},{80,32},{96,16},{112,0},{1... | collective-permute-start | bytes 122888 | tf_op jit(solution)/shard_map/ppermute | solution.py:173
  47.9 1.4 %collective-permute-done.4 = bf16[32,640]{1,0:T(8,128)(2,1)S(1)} collective-permute-done((bf16[32,640]{1,0:T(8,128)(2,1)S(1)}, bf16[32,640]{1,0:T(8,128)(2,1)S(1)}, u32[]{:S(2)}, u32[]{:S(2)}) %collective-permute-start.4) | collective-permute-done | bytes 40992 | tf_op jit(solution)/shard_map/ppermute | solution.py:173
  49.3 11.8 %all_to_all.16.own_ref = bf16[16,32,512]{2,1,0:T(8,128)(2,1)S(1)} all-to-all(bf16[16,32,512]{2,1,0:T(8,128)(2,1)S(1)} %broadcast_in_dim.15), channel_id=1, replica_groups=mesh['xh'=2,'z'=8,'xl'=2,'y'=4,'c'=2] {'xl','xh','y'}, dimensions={0} | all-to-all | bytes 1048576 | tf_op jit(solution)/shard_map/all_to_all | solution.py:240
  61.1 4.5 %collective-permute-start.5 = (bf16[16,32,512]{2,1,0:T(8,128)(2,1)S(1)}, bf16[16,32,512]{2,1,0:T(8,128)(2,1)S(1)}, u32[]{:S(2)}, u32[]{:S(2)}) collective-permute-start(bf16[16,32,512]{2,1,0:T(8,128)(2,1)S(1)} %all_to_all.16.own_ref), channel_id=1, source_target_pairs={{0,1},{1,0},{2,3},{3,2},{4,5},{5,4},{6,7},{7,6},{8,9},{9,8},{10,11... | collective-permute-start | bytes 1572872 | tf_op jit(solution)/shard_map/ppermute | solution.py:173
  65.6 0.0 collective-permute-start.6
  65.6 1.0 %shard_map.148 = (f32[512,512]{1,0:T(8,128)}, f32[512,512]{1,0:T(8,128)}, f32[8,32]{1,0:T(8,128)}) custom-call(bf16[16,32,512]{2,1,0:T(8,128)(2,1)S(1)} %all_to_all.16.own_ref, bf16[32,640]{1,0:T(8,128)(2,1)S(1)} %add_convert_fusion.sums_ref), custom_call_target="tpu_custom_call" | custom-call | flops 1048576 | bytes 2097152 | tf_op jit(solution)/shard_map/pallas_call | solution.py:245
  66.7 0.5 collective-permute-done.6.other_small_ref
  67.2 0.0 collective-permute-done.5.other_ref
  67.2 1.1 %shard_map.149 = (f32[512,512]{1,0:T(8,128)}, f32[512,512]{1,0:T(8,128)}, f32[3,512]{1,0:T(4,128)}, f32[1,512]{1,0:T(1,128)}, f32[1,512]{1,0:T(1,128)}, /*index=5*/f32[1,512]{1,0:T(1,128)}) custom-call(bf16[16,32,512]{2,1,0:T(8,128)(2,1)S(1)} %collective-permute-done.5.other_ref, ...), custom_call_target="tpu_custom_call", output_to_operand_aliasing={{0}: (3, {}), {1}: (4, {})} | custom-call | flops 1048576 | bytes 2097152 | tf_op jit(solution)/shard_map/pallas_call | solution.py:254
  (5 shorter events, 0.1 us)
Async XLA Ops:
  2.2 11.8 %all-to-all-start = ((bf16[8,8,1536]{2,1,0:T(8,128)(2,1)}), bf16[8,8,1536]{2,1,0:T(8,128)(2,1)S(1)}, u32[]{:S(2)}, u32[]{:S(2)}) async-start(bf16[8,8,1536]{2,1,0:T(8,128)(2,1)} %shard_map.144), calls=%async_computation | async-start | bytes 393216 | tf_op jit(solution)/shard_map/all_to_all | solution.py:191
  14.1 3.2 %collective-permute-start = (bf16[64,1536]{1,0:T(8,128)(2,1)S(1)}, bf16[64,1536]{1,0:T(8,128)(2,1)S(1)}, u32[]{:S(2)}, u32[]{:S(2)}) collective-permute-start(bf16[64,1536]{1,0:T(8,128)(2,1)S(1)} %bitcast.7), channel_id=1, source_target_pairs={{0,1},{1,0},{2,3},{3,2},{4,5},{5,4},{6,7},{7,6},{8,9},{9,8},{10,11... | collective-permute-start | bytes 589832 | tf_op jit(solution)/shard_map/ppermute | solution.py:173
  36.1 5.8 %collective-permute-start.3 = (bf16[32,640]{1,0:T(8,128)(2,1)S(1)}, bf16[32,640]{1,0:T(8,128)(2,1)S(1)}, u32[]{:S(2)}, u32[]{:S(2)}) collective-permute-start(bf16[32,640]{1,0:T(8,128)(2,1)S(1)} %reduce_sum.12), channel_id=1, source_target_pairs={{0,48},{16,32},{32,16},{48,0},{64,112},{80,96},{96,80},{112,64},{1... | collective-permute-start | bytes 122888 | tf_op jit(solution)/shard_map/ppermute | solution.py:173
  40.6 3.8 %collective-permute-start.2 = (bf16[32,640]{1,0:T(8,128)(2,1)S(1)}, bf16[32,640]{1,0:T(8,128)(2,1)S(1)}, u32[]{:S(2)}, u32[]{:S(2)}) collective-permute-start(bf16[32,640]{1,0:T(8,128)(2,1)S(1)} %reduce_sum.12), channel_id=1, source_target_pairs={{0,32},{16,48},{32,0},{48,16},{64,96},{80,112},{96,64},{112,80},{1... | collective-permute-start | bytes 122888 | tf_op jit(solution)/shard_map/ppermute | solution.py:173
  40.6 3.8 %collective-permute-start.1 = (bf16[32,640]{1,0:T(8,128)(2,1)S(1)}, bf16[32,640]{1,0:T(8,128)(2,1)S(1)}, u32[]{:S(2)}, u32[]{:S(2)}) collective-permute-start(bf16[32,640]{1,0:T(8,128)(2,1)S(1)} %reduce_sum.12), channel_id=1, source_target_pairs={{0,16},{16,0},{32,48},{48,32},{64,80},{80,64},{96,112},{112,96},{1... | collective-permute-start | bytes 122888 | tf_op jit(solution)/shard_map/ppermute | solution.py:173
  44.3 4.9 %collective-permute-start.4 = (bf16[32,640]{1,0:T(8,128)(2,1)S(1)}, bf16[32,640]{1,0:T(8,128)(2,1)S(1)}, u32[]{:S(2)}, u32[]{:S(2)}) collective-permute-start(bf16[32,640]{1,0:T(8,128)(2,1)S(1)} %add_convert_fusion.1), channel_id=1, source_target_pairs={{0,112},{16,96},{32,80},{48,64},{64,48},{80,32},{96,16},{112,0},{1... | collective-permute-start | bytes 122888 | tf_op jit(solution)/shard_map/ppermute | solution.py:173
  61.1 6.0 %collective-permute-start.5 = (bf16[16,32,512]{2,1,0:T(8,128)(2,1)S(1)}, bf16[16,32,512]{2,1,0:T(8,128)(2,1)S(1)}, u32[]{:S(2)}, u32[]{:S(2)}) collective-permute-start(bf16[16,32,512]{2,1,0:T(8,128)(2,1)S(1)} %all_to_all.16.own_ref), channel_id=1, source_target_pairs={{0,1},{1,0},{2,3},{3,2},{4,5},{5,4},{6,7},{7,6},{8,9},{9,8},{10,11... | collective-permute-start | bytes 1572872 | tf_op jit(solution)/shard_map/ppermute | solution.py:173
  65.6 1.5 %collective-permute-start.6 = (bf16[16,128]{1,0:T(8,128)(2,1)S(1)}, bf16[16,128]{1,0:T(8,128)(2,1)S(1)}, u32[]{:S(2)}, u32[]{:S(2)}) collective-permute-start(bf16[16,128]{1,0:T(8,128)(2,1)S(1)} %slice.9.own_small_ref), channel_id=1, source_target_pairs={{0,1},{1,0},{2,3},{3,2},{4,5},{5,4},{6,7},{7,6},{8,9},{9,8},{10,11... | collective-permute-start | bytes 12296 | tf_op jit(solution)/shard_map/ppermute | solution.py:173

commit v5 on v4

--- a/solution.py
+++ b/solution.py
@@ -101,8 +101,8 @@
     points = one_ref.shape[1]
     half = w_second_ref.shape[0] // 2
     own = pl.ds(pl.multiple_of(core * half, half), half)
-    grad_basis = tn(near_ref[:, points:], near_ref[:, :points])
-    grad_basis = grad_basis + tn(far_ref[:, points:], far_ref[:, :points])
+    both = jnp.concatenate([near_ref[...], far_ref[...]], axis=0)
+    grad_basis = tn(both[:, points:], both[:, :points])
     grad_basis_ref[...] = grad_basis.astype(BF16)
     two = two_ref[...].astype(F32)
     pre_two_ref[...] = (nn(w_third_ref[...], grad_basis_ref[...]) * (1.0 - two * two)).astype(BF16)

time: 68.5 us -> 68.2 us (level)
  no operation moved by 1% of the time
where the time goes in v5:
time: 68.2 us; the launch traced here: 67.9 us
  blocking collectives  28.1 us (41%)
  starting transfers between devices  20.8 us (30%)
  Pallas kernels  10.3 us (15%)
  waiting for transfers between devices  7.76 us (11%)
  between operations  0.71 us (1%)
    all_to_all x1, blocking collectives, shards(): parts = lax.all_to_all(partial, PLANE, 0, 0, tiled=True)  16.4 us
    ppermute x7, starting transfers between devices, swap(): lax.ppermute(value, axis, [(i, i ^ bits) for i in range(dict(SPLIT)[axis])])  14.9 us
    all_to_all x1, blocking collectives, shards(): gathered = lax.all_to_all(gathered, PLANE, 0, 0, tiled=True)  11.7 us
    all_to_all x1, starting transfers between devices, shards(): lax.all_to_all(send, ('xl', 'y'), 0, 0, tiled=True)  5.95 us
    ppermute x7, waiting for transfers between devices, swap(): lax.ppermute(value, axis, [(i, i ^ bits) for i in range(dict(SPLIT)[axis])])  5.26 us
    pallas_call x1, Pallas kernels, shards(): pl.pallas_call(forward_kernel, out_shape=(pltpu.VMEM((2, 512, points), BF...  3.37 us
    all_to_all x1, waiting for transfers between devices, shards(): lax.all_to_all(send, ('xl', 'y'), 0, 0, tiled=True)  2.5 us
    pallas_call x1, Pallas kernels, shards(): pl.pallas_call(backward_kernel, out_shape=jax.ShapeDtypeStruct((16, 32, 6...  2.06 us
  transfers between devices with their start and end apart: 8, of which 5 were waited for; matrix products, arithmetic and copies ran while one was open for 0% of the time, Pallas kernels for 8%

profile of v5, /device:TPU:1, one launch (start us, length us, event | category | flops | bytes accessed | tf_op | source)
XLA Modules:
  0.0 67.9 jit_solution(15104010948824201087)
XLA Ops:
  0.6 1.6 %shard_map.144 = bf16[8,8,1536]{2,1,0:T(8,128)(2,1)} custom-call(bf16[8,8192]{1,0:T(8,128)(2,1)} %grad_out_ref.1, bf16[8,512]{1,0:T(8,128)(2,1)} %coef_ref.1), custom_call_target="tpu_custom_call" | custom-call | tf_op jit(solution)/shard_map/pallas_call | solution.py:185
  2.2 5.9 %all-to-all-start = ((bf16[8,8,1536]{2,1,0:T(8,128)(2,1)}), bf16[8,8,1536]{2,1,0:T(8,128)(2,1)S(1)}, u32[]{:S(2)}, u32[]{:S(2)}) async-start(bf16[8,8,1536]{2,1,0:T(8,128)(2,1)} %shard_map.144), calls=%async_computation | async-start | bytes 393216 | tf_op jit(solution)/shard_map/all_to_all | solution.py:191
  8.2 3.4 %shard_map.145 = (bf16[2,512,1024]{2,1,0:T(8,128)(2,1)S(1)}, bf16[512,1024]{1,0:T(8,128)(2,1)S(1)}, f32[3,1024]{1,0:T(4,128)S(1)}) custom-call(f32[3,8192]{1,0:T(4,128)} %coords_ref.1, f32[3,512]{1,0:T(4,128)} %w_first_ref.1, f32[1,512]{1,0:T(1,128)} %bitcast.10, bf16[512,512]{1,0:T(8,128)(2,1)} %w_second_ref.3, f32[1,512]{1,0:T(1,128)} %bitcast.11, ...), custom_call_target="tpu_custom_call" | custom-call | flops 1073741824 | bytes 5242880 | tf_op jit(solution)/shard_map/pallas_call | solution.py:192
  11.6 2.5 %all-to-all-done = bf16[8,8,1536]{2,1,0:T(8,128)(2,1)S(1)} async-done(((bf16[8,8,1536]{2,1,0:T(8,128)(2,1)}), bf16[8,8,1536]{2,1,0:T(8,128)(2,1)S(1)}, u32[]{:S(2)}, u32[]{:S(2)}) %all-to-all-start) | async-done | bytes 196640 | tf_op jit(solution)/shard_map/all_to_all | solution.py:191
  14.1 2.0 %collective-permute-start = (bf16[64,1536]{1,0:T(8,128)(2,1)S(1)}, bf16[64,1536]{1,0:T(8,128)(2,1)S(1)}, u32[]{:S(2)}, u32[]{:S(2)}) collective-permute-start(bf16[64,1536]{1,0:T(8,128)(2,1)S(1)} %bitcast.7), channel_id=1, source_target_pairs={{0,1},{1,0},{2,3},{3,2},{4,5},{5,4},{6,7},{7,6},{8,9},{9,8},{10,11... | collective-permute-start | bytes 589832 | tf_op jit(solution)/shard_map/ppermute | solution.py:173
  16.1 1.2 %shard_map.146 = (f32[64,512]{1,0:T(8,128)S(1)}, bf16[2,512,512]{2,1,0:T(8,128)(2,1)S(1)}) custom-call(bf16[64,1536]{1,0:T(8,128)(2,1)S(1)} %bitcast.8, bf16[512,1024]{1,0:T(8,128)(2,1)S(1)} %get-tuple-element.26.basis_ref, bf16[512,512]{1,0:T(8,128)(2,1)} %w_second_ref.3, bf16[512,512]{1,0:T(8,128)(2,1)} %w_third_ref.3), custom_call_target="tpu_custom_call" | custom-call | flops 268435456 | bytes 2097152 | tf_op jit(solution)/shard_map/pallas_call | solution.py:212
  17.3 0.0 collective-permute-done.far_ref
  17.3 2.1 %shard_map.147 = bf16[16,32,640]{2,1,0:T(8,128)(2,1)S(1)} custom-call(bf16[64,1536]{1,0:T(8,128)(2,1)S(1)} %bitcast.9, bf16[64,1536]{1,0:T(8,128)(2,1)S(1)} %collective-permute-done.far_ref, f32[3,1024]{1,0:T(4,128)S(1)} %get-tuple-element.25.xyz_ref, bf16[2,512,512]{2,1,0:T(8,128)(2,1)S(1)} %get-tuple-element.27.weights_ref, ...), custom_call_target="tpu_custom_call" | custom-call | flops 2147483648 | bytes 5242880 | tf_op jit(solution)/shard_map/pallas_call | solution.py:221
  19.4 16.4 %all_to_all.15 = bf16[16,32,640]{2,1,0:T(8,128)(2,1)S(1)} all-to-all(bf16[16,32,640]{2,1,0:T(8,128)(2,1)S(1)} %shard_map.147), channel_id=1, replica_groups=mesh['xh'=2,'z'=8,'xl'=2,'y'=4,'c'=2] {'xl','xh','y'}, dimensions={0} | all-to-all | bytes 1310720 | tf_op jit(solution)/shard_map/all_to_all | solution.py:231
  35.8 0.1 reduce_sum.12
  35.9 4.4 %collective-permute-start.3 = (bf16[32,640]{1,0:T(8,128)(2,1)S(1)}, bf16[32,640]{1,0:T(8,128)(2,1)S(1)}, u32[]{:S(2)}, u32[]{:S(2)}) collective-permute-start(bf16[32,640]{1,0:T(8,128)(2,1)S(1)} %reduce_sum.12), channel_id=1, source_target_pairs={{0,48},{16,32},{32,16},{48,0},{64,112},{80,96},{96,80},{112,64},{1... | collective-permute-start | bytes 122888 | tf_op jit(solution)/shard_map/ppermute | solution.py:173
  40.3 0.0 collective-permute-start.2
  40.3 0.4 collective-permute-start.1
  40.7 1.0 %collective-permute-done.3 = bf16[32,640]{1,0:T(8,128)(2,1)S(1)} collective-permute-done((bf16[32,640]{1,0:T(8,128)(2,1)S(1)}, bf16[32,640]{1,0:T(8,128)(2,1)S(1)}, u32[]{:S(2)}, u32[]{:S(2)}) %collective-permute-start.3) | collective-permute-done | bytes 40992 | tf_op jit(solution)/shard_map/ppermute | solution.py:173
  41.7 2.4 %collective-permute-done.2 = bf16[32,640]{1,0:T(8,128)(2,1)S(1)} collective-permute-done((bf16[32,640]{1,0:T(8,128)(2,1)S(1)}, bf16[32,640]{1,0:T(8,128)(2,1)S(1)}, u32[]{:S(2)}, u32[]{:S(2)}) %collective-permute-start.2) | collective-permute-done | bytes 40992 | tf_op jit(solution)/shard_map/ppermute | solution.py:173
  44.0 0.0 collective-permute-done.1
  44.1 3.5 %collective-permute-start.4 = (bf16[32,640]{1,0:T(8,128)(2,1)S(1)}, bf16[32,640]{1,0:T(8,128)(2,1)S(1)}, u32[]{:S(2)}, u32[]{:S(2)}) collective-permute-start(bf16[32,640]{1,0:T(8,128)(2,1)S(1)} %add_convert_fusion.1), channel_id=1, source_target_pairs={{0,112},{16,96},{32,80},{48,64},{64,48},{80,32},{96,16},{112,0},{1... | collective-permute-start | bytes 122888 | tf_op jit(solution)/shard_map/ppermute | solution.py:173
  47.6 1.4 %collective-permute-done.4 = bf16[32,640]{1,0:T(8,128)(2,1)S(1)} collective-permute-done((bf16[32,640]{1,0:T(8,128)(2,1)S(1)}, bf16[32,640]{1,0:T(8,128)(2,1)S(1)}, u32[]{:S(2)}, u32[]{:S(2)}) %collective-permute-start.4) | collective-permute-done | bytes 40992 | tf_op jit(solution)/shard_map/ppermute | solution.py:173
  49.1 11.7 %all_to_all.16.own_ref = bf16[16,32,512]{2,1,0:T(8,128)(2,1)S(1)} all-to-all(bf16[16,32,512]{2,1,0:T(8,128)(2,1)S(1)} %broadcast_in_dim.15), channel_id=1, replica_groups=mesh['xh'=2,'z'=8,'xl'=2,'y'=4,'c'=2] {'xl','xh','y'}, dimensions={0} | all-to-all | bytes 1048576 | tf_op jit(solution)/shard_map/all_to_all | solution.py:240
  60.8 4.5 %collective-permute-start.5 = (bf16[16,32,512]{2,1,0:T(8,128)(2,1)S(1)}, bf16[16,32,512]{2,1,0:T(8,128)(2,1)S(1)}, u32[]{:S(2)}, u32[]{:S(2)}) collective-permute-start(bf16[16,32,512]{2,1,0:T(8,128)(2,1)S(1)} %all_to_all.16.own_ref), channel_id=1, source_target_pairs={{0,1},{1,0},{2,3},{3,2},{4,5},{5,4},{6,7},{7,6},{8,9},{9,8},{10,11... | collective-permute-start | bytes 1572872 | tf_op jit(solution)/shard_map/ppermute | solution.py:173
  65.3 0.0 collective-permute-start.6
  65.3 1.0 %shard_map.148 = (f32[512,512]{1,0:T(8,128)}, f32[512,512]{1,0:T(8,128)}, f32[8,32]{1,0:T(8,128)}) custom-call(bf16[16,32,512]{2,1,0:T(8,128)(2,1)S(1)} %all_to_all.16.own_ref, bf16[32,640]{1,0:T(8,128)(2,1)S(1)} %add_convert_fusion.sums_ref), custom_call_target="tpu_custom_call" | custom-call | flops 1048576 | bytes 2097152 | tf_op jit(solution)/shard_map/pallas_call | solution.py:245
  66.4 0.5 collective-permute-done.6.other_small_ref
  66.9 0.0 collective-permute-done.5.other_ref
  66.9 1.1 %shard_map.149 = (f32[512,512]{1,0:T(8,128)}, f32[512,512]{1,0:T(8,128)}, f32[3,512]{1,0:T(4,128)}, f32[1,512]{1,0:T(1,128)}, f32[1,512]{1,0:T(1,128)}, /*index=5*/f32[1,512]{1,0:T(1,128)}) custom-call(bf16[16,32,512]{2,1,0:T(8,128)(2,1)S(1)} %collective-permute-done.5.other_ref, ...), custom_call_target="tpu_custom_call", output_to_operand_aliasing={{0}: (3, {}), {1}: (4, {})} | custom-call | flops 1048576 | bytes 2097152 | tf_op jit(solution)/shard_map/pallas_call | solution.py:254
  (5 shorter events, 0.1 us)
Async XLA Ops:
  2.2 11.8 %all-to-all-start = ((bf16[8,8,1536]{2,1,0:T(8,128)(2,1)}), bf16[8,8,1536]{2,1,0:T(8,128)(2,1)S(1)}, u32[]{:S(2)}, u32[]{:S(2)}) async-start(bf16[8,8,1536]{2,1,0:T(8,128)(2,1)} %shard_map.144), calls=%async_computation | async-start | bytes 393216 | tf_op jit(solution)/shard_map/all_to_all | solution.py:191
  14.1 3.2 %collective-permute-start = (bf16[64,1536]{1,0:T(8,128)(2,1)S(1)}, bf16[64,1536]{1,0:T(8,128)(2,1)S(1)}, u32[]{:S(2)}, u32[]{:S(2)}) collective-permute-start(bf16[64,1536]{1,0:T(8,128)(2,1)S(1)} %bitcast.7), channel_id=1, source_target_pairs={{0,1},{1,0},{2,3},{3,2},{4,5},{5,4},{6,7},{7,6},{8,9},{9,8},{10,11... | collective-permute-start | bytes 589832 | tf_op jit(solution)/shard_map/ppermute | solution.py:173
  35.9 5.8 %collective-permute-start.3 = (bf16[32,640]{1,0:T(8,128)(2,1)S(1)}, bf16[32,640]{1,0:T(8,128)(2,1)S(1)}, u32[]{:S(2)}, u32[]{:S(2)}) collective-permute-start(bf16[32,640]{1,0:T(8,128)(2,1)S(1)} %reduce_sum.12), channel_id=1, source_target_pairs={{0,48},{16,32},{32,16},{48,0},{64,112},{80,96},{96,80},{112,64},{1... | collective-permute-start | bytes 122888 | tf_op jit(solution)/shard_map/ppermute | solution.py:173
  40.3 3.8 %collective-permute-start.2 = (bf16[32,640]{1,0:T(8,128)(2,1)S(1)}, bf16[32,640]{1,0:T(8,128)(2,1)S(1)}, u32[]{:S(2)}, u32[]{:S(2)}) collective-permute-start(bf16[32,640]{1,0:T(8,128)(2,1)S(1)} %reduce_sum.12), channel_id=1, source_target_pairs={{0,32},{16,48},{32,0},{48,16},{64,96},{80,112},{96,64},{112,80},{1... | collective-permute-start | bytes 122888 | tf_op jit(solution)/shard_map/ppermute | solution.py:173
  40.3 3.8 %collective-permute-start.1 = (bf16[32,640]{1,0:T(8,128)(2,1)S(1)}, bf16[32,640]{1,0:T(8,128)(2,1)S(1)}, u32[]{:S(2)}, u32[]{:S(2)}) collective-permute-start(bf16[32,640]{1,0:T(8,128)(2,1)S(1)} %reduce_sum.12), channel_id=1, source_target_pairs={{0,16},{16,0},{32,48},{48,32},{64,80},{80,64},{96,112},{112,96},{1... | collective-permute-start | bytes 122888 | tf_op jit(solution)/shard_map/ppermute | solution.py:173
  44.1 4.9 %collective-permute-start.4 = (bf16[32,640]{1,0:T(8,128)(2,1)S(1)}, bf16[32,640]{1,0:T(8,128)(2,1)S(1)}, u32[]{:S(2)}, u32[]{:S(2)}) collective-permute-start(bf16[32,640]{1,0:T(8,128)(2,1)S(1)} %add_convert_fusion.1), channel_id=1, source_target_pairs={{0,112},{16,96},{32,80},{48,64},{64,48},{80,32},{96,16},{112,0},{1... | collective-permute-start | bytes 122888 | tf_op jit(solution)/shard_map/ppermute | solution.py:173
  60.8 6.1 %collective-permute-start.5 = (bf16[16,32,512]{2,1,0:T(8,128)(2,1)S(1)}, bf16[16,32,512]{2,1,0:T(8,128)(2,1)S(1)}, u32[]{:S(2)}, u32[]{:S(2)}) collective-permute-start(bf16[16,32,512]{2,1,0:T(8,128)(2,1)S(1)} %all_to_all.16.own_ref), channel_id=1, source_target_pairs={{0,1},{1,0},{2,3},{3,2},{4,5},{5,4},{6,7},{7,6},{8,9},{9,8},{10,11... | collective-permute-start | bytes 1572872 | tf_op jit(solution)/shard_map/ppermute | solution.py:173
  65.3 1.5 %collective-permute-start.6 = (bf16[16,128]{1,0:T(8,128)(2,1)S(1)}, bf16[16,128]{1,0:T(8,128)(2,1)S(1)}, u32[]{:S(2)}, u32[]{:S(2)}) collective-permute-start(bf16[16,128]{1,0:T(8,128)(2,1)S(1)} %slice.9.own_small_ref), channel_id=1, source_target_pairs={{0,1},{1,0},{2,3},{3,2},{4,5},{5,4},{6,7},{7,6},{8,9},{9,8},{10,11... | collective-permute-start | bytes 12296 | tf_op jit(solution)/shard_map/ppermute | solution.py:173
